TPU v7x, 256 devices: a whole 4x4x8 slice. The times are simulated.
256 devices in a mesh: expert: 16 (over z, core), tensor: 16 (over y, x).
Axes of the slice: x: 4, y: 4, z: 8, core: 2. Of those that a mesh axis runs over, the one named last changes fastest.
Arguments:
- hidden_in: bfloat16 [256, 4096], P(('expert', 'tensor')), may hold values from -6 to 6
- x_stream: bfloat16 [256, 8192], P('expert', 'tensor'), may hold values from -6 to 6
- z_stream: bfloat16 [256, 8192], P('expert', 'tensor'), may hold values from -6 to 6
- conv_state: bfloat16 [256, 3, 8192], P('expert', None, 'tensor'), may hold values from -6 to 6
- ssm_state: float32 [256, 16, 8192], P('expert', None, 'tensor'), may hold values from -3 to 3
- conv_weight: bfloat16 [4, 8192], P(None, 'tensor'), may hold values from -3 to 3
- conv_bias: float32 [8192], P('tensor'), may hold values from -3 to 3
- x_weight: bfloat16 [8192, 544], P('tensor'), may hold values from -0.0625 to 0.0625
- dt_weight: bfloat16 [512, 8192], P(None, 'tensor'), may hold values from -0.25 to 0.25
- dt_bias: float32 [8192], P('tensor'), may hold values from -4 to -1
- a_log: float32 [16, 8192], P(None, 'tensor'), may hold values from 0 to 2.8
- skip_gain: float32 [8192], P('tensor'), may hold values from 0.5 to 1.5
- out_weight: bfloat16 [16, 512, 4096], P('tensor', 'expert'), may hold values from -0.0625 to 0.0625
- norm_gain: float32 [4096], replicated, may hold values from 0.5 to 1.5
- route_ids: int32 [256, 2], replicated, may hold values from 0 to 7, as said below
- route_weights: float32 [256, 2], replicated, may hold values from 0.1 to 0.9
- gate_proj: bfloat16 [16, 4096, 6144], P('expert', None, 'tensor'), may hold values from -0.09375 to 0.09375
- up_proj: bfloat16 [16, 4096, 6144], P('expert', None, 'tensor'), may hold values from -0.09375 to 0.09375
- down_proj: bfloat16 [16, 6144, 4096], P('expert', 'tensor'), may hold values from -0.0546875 to 0.0546875
Outputs:
- layer_output: bfloat16 [256, 4096], P(('expert', 'tensor'))
- new_conv_state: bfloat16 [256, 3, 8192], P('expert', None, 'tensor')
- new_ssm_state: float32 [256, 16, 8192], P('expert', None, 'tensor')
Inputs may be any that keep to these rules, and one draw needn't show every extreme that they name: `route_ids`: each request names two different experts. Among the 16 requests of each index of expert (rows g * 16 to (g + 1) * 16 - 1) no expert is named more than 12 times, and one expert, the same for every index, is named exactly 12 times.
All inputs are finite; a program needn't handle non-finite values.
Results may differ from a plain program's by a relative error of at most 0.025.
Values may be sent and summed in bfloat16 or wider, within the bound.
A program may use at most 64 MiB of HBM per device.

v0:
```python
import jax
import jax.numpy as jnp
from jax import lax
from jax.sharding import PartitionSpec as P

EXPERTS = 8


def rms_norm(values, gain):
    wide = values.astype(jnp.float32)
    scale = lax.rsqrt(jnp.mean(wide * wide, axis=-1, keepdims=True) + 1e-05)
    return (wide * scale * gain).astype(jnp.bfloat16)


def expert_mlp(rows_in, w_gate, w_up, w_down):
    gate_part = jnp.dot(rows_in, w_gate, preferred_element_type=jnp.float32)
    up_part = jnp.dot(rows_in, w_up, preferred_element_type=jnp.float32)
    active = (jax.nn.silu(gate_part) * up_part).astype(jnp.bfloat16)
    return jnp.dot(active, w_down, preferred_element_type=jnp.float32)


def local(
    hidden_in,
    x_stream,
    z_stream,
    conv_state,
    ssm_state,
    conv_weight,
    conv_bias,
    x_weight,
    dt_weight,
    dt_bias,
    a_log,
    skip_gain,
    out_weight,
    norm_gain,
    route_ids,
    route_weights,
    gate_proj,
    up_proj,
    down_proj,
):
    window = jnp.concatenate([conv_state, x_stream[:, None, :]], axis=1)
    conv_sum = (
        jnp.sum(window.astype(jnp.float32) * conv_weight.astype(jnp.float32)[None], axis=1)
        + conv_bias
    )
    conv_out = jax.nn.silu(conv_sum).astype(jnp.bfloat16)
    new_conv_state = window[:, 1:, :]
    partial_proj = jnp.dot(conv_out, x_weight, preferred_element_type=jnp.float32)
    selective = lax.psum(partial_proj.astype(jnp.bfloat16), "tensor").astype(jnp.float32)
    rank_low = dt_weight.shape[0]
    state_size = a_log.shape[0]
    dt_low = selective[:, :rank_low].astype(jnp.bfloat16)
    b_part = selective[:, rank_low : rank_low + state_size]
    c_part = selective[:, rank_low + state_size :]
    step_size = jax.nn.softplus(
        jnp.dot(dt_low, dt_weight, preferred_element_type=jnp.float32) + dt_bias
    )
    decay_rate = jnp.exp(-step_size[:, None, :] * jnp.exp(a_log)[None])
    inputs = conv_out.astype(jnp.float32)
    new_ssm_state = decay_rate * ssm_state + (step_size * inputs)[:, None, :] * b_part[:, :, None]
    readout = jnp.sum(new_ssm_state * c_part[:, :, None], axis=1) + skip_gain * inputs
    mixer_out = (readout * jax.nn.silu(z_stream.astype(jnp.float32))).astype(jnp.bfloat16)
    arrived = lax.all_to_all(mixer_out, "expert", split_axis=1, concat_axis=0, tiled=True)
    mixed_sum = lax.psum_scatter(
        jnp.dot(arrived, out_weight[0], preferred_element_type=jnp.float32),
        ("expert", "tensor"),
        scatter_dimension=0,
        tiled=True,
    )
    residual = (hidden_in.astype(jnp.float32) + mixed_sum).astype(jnp.bfloat16)
    normed = rms_norm(residual, norm_gain)
    expert_count = lax.axis_size("expert")
    halves = expert_count // EXPERTS
    total_rows = route_ids.shape[0]
    group_size = total_rows // expert_count
    slot_count = 3 * group_size // 4
    everyone = lax.all_gather(normed, ("expert", "tensor"), axis=0, tiled=True)
    capacity = slot_count * expert_count
    expert = lax.axis_index("expert") // halves
    hit_mask = route_ids == expert
    member = jnp.any(hit_mask, axis=1)
    weight = jnp.sum(jnp.where(hit_mask, route_weights, 0.0), axis=1)
    slot_place = jnp.cumsum(member.astype(jnp.int32)) - 1
    target = jnp.where(member, slot_place, capacity)
    row_ids = jnp.arange(total_rows, dtype=jnp.int32)
    slot_rows = jnp.zeros((capacity + 1,), jnp.int32).at[target].set(row_ids)[:capacity]
    result = expert_mlp(everyone[slot_rows], gate_proj[0], up_proj[0], down_proj[0])
    gathered = result[jnp.clip(slot_place, 0, capacity - 1)]
    expert_total = lax.psum_scatter(
        jnp.where(member[:, None], weight[:, None] * gathered, 0.0),
        ("expert", "tensor"),
        scatter_dimension=0,
        tiled=True,
    )
    layer_output = (residual.astype(jnp.float32) + expert_total).astype(jnp.bfloat16)
    return (layer_output, new_conv_state, new_ssm_state)


def solution(mesh):
    return jax.shard_map(
        local,
        mesh=mesh,
        in_specs=(
            P(("expert", "tensor"), None),
            P("expert", "tensor"),
            P("expert", "tensor"),
            P("expert", None, "tensor"),
            P("expert", None, "tensor"),
            P(None, "tensor"),
            P("tensor"),
            P("tensor", None),
            P(None, "tensor"),
            P("tensor"),
            P(None, "tensor"),
            P("tensor"),
            P("tensor", "expert", None),
            P(),
            P(),
            P(),
            P("expert", None, "tensor"),
            P("expert", None, "tensor"),
            P("expert", "tensor", None),
        ),
        out_specs=(
            P(("expert", "tensor"), None),
            P("expert", None, "tensor"),
            P("expert", None, "tensor"),
        ),
        check_vma=False,
    )
```

profile of v0, /device:TPU:1, one launch (start us, length us, event | category | flops | bytes accessed | tf_op | source)
XLA Modules:
  0.0 794.7 jit_solution(4352064692092446053)
XLA Ops:
  7.2 0.9 convert_element_type.53
  8.1 0.9 multiply_reduce_fusion.1
  9.0 1.3 convolution_convert_fusion
  10.4 61.3 %psum.7 = bf16[16,544]{1,0:T(8,128)(2,1)S(1)} all-reduce(bf16[16,544]{1,0:T(8,128)(2,1)S(1)} %convolution_convert_fusion), channel_id=1, replica_groups=mesh['expert'=16,'tensor'=16] {'tensor'}, use_global_device_ids=true, to_apply=%region_1.2 | all-reduce | flops 8704 | bytes 34816 | tf_op jit(solution)/shard_map/psum | solution.py:51
  71.7 0.8 exp.23
  72.5 1.3 fusion.38
  73.8 2.1 multiply_reduce_fusion
  75.8 0.8 fusion.25
  76.6 0.1 all_to_all.14
  76.7 0.1 reshape.136
  76.8 30.5 %all_to_all.19 = bf16[16,2,256]{2,1,0:T(2,128)(2,1)S(1)} all-to-all(bf16[16,2,256]{2,1,0:T(2,128)(2,1)S(1)} %reshape.136), channel_id=1, replica_groups=mesh['expert'=16,'tensor'=16] {'expert'}, dimensions={0} | all-to-all | bytes 32768 | tf_op jit(solution)/shard_map/all_to_all | solution.py:65
  107.3 0.1 reshape.137
  107.4 2.7 fusion.19
  110.2 258.1 %all-reduce.5.cloned.1.call-done = f32[256,4096]{1,0:T(8,128)} async-done(((f32[256,4096]{1,0:T(8,128)}), f32[256,4096]{1,0:T(8,128)}) %all-reduce.5.cloned.1.call-update) | async-done | bytes 4194320
  368.3 1.5 multiply_reduce_fusion.2
  370.5 0.6 convert_bitcast_fusion
  371.3 0.3 reduce-window.9
  371.6 0.1 slice.26
  371.7 0.1 slice_reduce_fusion
  371.8 0.1 add_add_fusion
  371.9 1.6 scatter_custom_fusion
  373.6 115.6 %all-gather.3.cloned.1.call-done = bf16[256,1,4096]{2,1,0:T(2,128)(2,1)} async-done(((bf16[1,1,4096]{2,1,0:T(2,128)(2,1)}), bf16[256,1,4096]{2,1,0:T(2,128)(2,1)}) %all-gather.3.cloned.1.call-update) | async-done | bytes 2097168 | tf_op jit(solution)/shard_map/all_gather | solution.py:79
  489.1 5.8 copy.28
  495.0 6.1 gather_fusion
  501.0 3.3 fusion.4
  504.4 5.9 fusion
  510.3 7.5 gather_fusion.1
  517.9 4.9 multiply_select_fusion
  522.8 0.8 copy-done.2
  523.6 0.6 fusion.22
  524.2 262.5 %all-reduce.7.cloned.1.call-done = f32[256,4096]{1,0:T(8,128)} async-done(((f32[256,4096]{1,0:T(8,128)}), f32[256,4096]{1,0:T(8,128)}) %all-reduce.7.cloned.1.call-update) | async-done | bytes 4194320
  786.7 1.5 fusion.30
  (32 shorter events, 0.4 us)
Async XLA Ops:
  7.2 497.2 %copy-start = (bf16[1,384,4096]{2,1,0:T(8,128)(2,1)S(1)}, bf16[1,384,4096]{2,1,0:T(8,128)(2,1)}, u32[]{:S(2)}) copy-start(bf16[1,384,4096]{2,1,0:T(8,128)(2,1)} %param.37) | copy-start | bytes 9437188
  7.2 100.2 %copy-start.1 = (bf16[1,32,4096]{2,1,0:T(8,128)(2,1)S(1)}, bf16[1,32,4096]{2,1,0:T(8,128)(2,1)}, u32[]{:S(2)}) copy-start(bf16[1,32,4096]{2,1,0:T(8,128)(2,1)} %param.31) | copy-start | bytes 786436
  7.2 361.1 %all-reduce.5.cloned.1.call-start = ((), (), s32[]{:S(2)}) async-start(), calls=%async_computation.2 | async-start | bytes 8388608
  110.1 258.2 %copy-start.4 = (bf16[1,4096]{1,0:T(2,128)(2,1)S(1)}, bf16[1,4096]{1,0:T(2,128)(2,1)}, u32[]{:S(2)}) copy-start(bf16[1,4096]{1,0:T(2,128)(2,1)} %param.19) | copy-start | bytes 24580
  110.1 260.4 %copy-start.5 = (f32[4096]{0:T(1024)S(1)}, f32[4096]{0:T(1024)}, u32[]{:S(2)}) copy-start(f32[4096]{0:T(1024)} %param.32) | copy-start | bytes 49156
  110.1 261.2 %copy-start.6 = (s32[256,2]{0,1:T(2,128)S(1)}, s32[256,2]{0,1:T(2,128)}, u32[]{:S(2)}) copy-start(s32[256,2]{0,1:T(2,128)} %param.33) | copy-start | bytes 6148
  110.1 263.4 %copy-start.7 = (f32[256,2]{0,1:T(2,128)S(1)}, f32[256,2]{0,1:T(2,128)}, u32[]{:S(2)}) copy-start(f32[256,2]{0,1:T(2,128)} %param.34) | copy-start | bytes 6148
  110.1 379.0 %all-gather.3.cloned.1.call-start = ((), (), s32[]{:S(2)}) async-start(), calls=%async_computation.1 | async-start | bytes 4210688 | tf_op jit(solution)/shard_map/all_gather | solution.py:79
  371.2 415.5 %all-reduce.7.cloned.1.call-start = ((), (), s32[]{:S(2)}) async-start(), calls=%async_computation.3 | async-start | bytes 8388608
  522.7 0.8 copy-start.2
  522.8 0.8 copy-start.3
Sparse Core Ops, SparseCore 0:
  110.2 257.9 all-reduce.4
  373.2 115.8 all-gather.2
  522.9 263.7 all-reduce.6
where the time goes:
time: 796 us; the launch traced here: 795 us
  waiting for transfers between devices  636 us (80%)
  blocking collectives  91.7 us (12%)
  local copies, waits for them, and re-layouts  23.2 us (3%)
  between operations  14.6 us (2%)
  matrix products  14.5 us (2%)
  other arithmetic  14.4 us (2%)
    unnamed x5, waiting for transfers between devices  521 us
    all_gather x1, waiting for transfers between devices, local(): everyone = lax.all_gather(normed, ('expert', 'tensor'), axis=0, tiled=True)  116 us
    psum x1, blocking collectives, local(): lax.psum(partial_proj.astype(jnp.bfloat16), 'tensor').astype(jnp.float32)  61.3 us
    all_to_all x1, blocking collectives, local(): lax.all_to_all(mixer_out, 'expert', split_axis=1, concat_axis=0, tiled=True)  30.5 us
  transfers between devices with their start and end apart: 3, of which 3 were waited for; matrix products, arithmetic and copies ran while one was open for 0% of the time, Pallas kernels for 0%

commit v1 on v0

v1 whole, which is shorter than its diff:
```python
import jax
import jax.numpy as jnp
from jax import lax
from jax.experimental import pallas as pl
from jax.experimental.pallas import tpu as pltpu
from jax.sharding import PartitionSpec as P

F32 = jnp.float32
BF16 = jnp.bfloat16
MESH = pl.DeviceIdType.MESH

PROJ_X, PROJ_Y, WOUT, HIDDEN, MIXED, OUTRED, RESID, ROWS1, ROWS2, ROWS3, PAIR, RED1, RED2, FINAL = range(14)


def layer_kernel(
    x_ref, z_ref, cs_ref, cw_ref, cb_ref, xw_ref, dtb_ref, alog_ref, skip_ref, gain_ref, ids_ref, rw_ref, hid_ref,
    dtw_hbm, ssm_hbm, ow_hbm, gate_hbm, up_hbm, down_hbm,
    out_ref, ncs_ref, nssm_ref,
    dtw, ssm, wg, wu, wd, ow,
    proj, proj_x, proj_y, hid_out, hid_in, readout, mix, outb, outr, res, resrow, xn, acc_g, acc_u, actw, wrow, perm,
    osend, opair, own, red1, tsum, red2, vrow, vsend, final_in,
    ssem, rsem, lsem,
):
    e = lax.axis_index("expert")
    t = lax.axis_index("tensor")
    y, x = lax.div(t, 4), lax.rem(t, 4)
    c = lax.rem(e, 2)
    mate = e + 1 - 2 * c
    expert = lax.div(e, 2)

    def rcopy(src, dst, phase, to, frm, device):
        return pltpu.make_async_remote_copy(
            src_ref=src, dst_ref=dst, send_sem=ssem.at[phase, to], recv_sem=rsem.at[phase, frm],
            device_id=device, device_id_type=MESH,
        )

    def others(n, me, body):
        def step(d, carry):
            body(lax.rem(me + d, n))
            return carry
        lax.fori_loop(1, n, step, 0)

    bar = pltpu.get_barrier_semaphore()
    others(16, e, lambda o: pl.semaphore_signal(bar, inc=1, device_id=(o, t), device_id_type=MESH))
    others(16, t, lambda o: pl.semaphore_signal(bar, inc=1, device_id=(e, o), device_id_type=MESH))

    def lcopy(src, dst, i):
        return pltpu.make_async_copy(src, dst, lsem.at[i])

    dtw_copy = lcopy(dtw_hbm, dtw, 0)
    ssm_copy = lcopy(ssm_hbm, ssm, 1)
    my_cols = pl.ds(pl.multiple_of(e * 256, 256), 256)
    ow_copy = lcopy(ow_hbm.at[0, :, my_cols], ow.at[e], 2)
    dtw_copy.start()
    ssm_copy.start()
    ow_copy.start()
    weights = []
    for q in range(4):
        weights.append((
            lcopy(gate_hbm.at[0, pl.ds(q * 1024, 1024), :], wg.at[q], 3 + q),
            lcopy(up_hbm.at[0, pl.ds(q * 1024, 1024), :], wu.at[q], 7 + q),
            lcopy(down_hbm.at[0, :, pl.ds(q * 1024, 1024)], wd.at[q], 11 + q),
        ))

    state = cs_ref[...].astype(F32)
    taps = cw_ref[...].astype(F32)
    newest = x_ref[...].astype(F32)
    window = [state[:, 0, :], state[:, 1, :], state[:, 2, :], newest]
    conv_sum = sum(window[k] * taps[k : k + 1, :] for k in range(4)) + cb_ref[...]
    conv_out = jax.nn.silu(conv_sum).astype(BF16)
    inputs = conv_out.astype(F32)
    part = jnp.dot(conv_out, xw_ref[...], preferred_element_type=F32)
    proj[0] = jnp.zeros((16, 640), BF16)
    proj[0, :, 0:544] = part.astype(BF16)

    pl.semaphore_wait(bar, 30)

    def proj_x_copy(o):
        return rcopy(proj.at[0], proj_x.at[x], PROJ_X, o, x, (e, y * 4 + o))

    others(4, x, lambda o: proj_x_copy(o).start())

    hidden = hid_ref[...].astype(F32)
    for k in range(16):
        hid_out[k] = hidden[:, 256 * k : 256 * (k + 1)]
    hid_in[e] = hid_out[e]

    def wout_copy(o):
        cols = pl.ds(pl.multiple_of(o * 256, 256), 256)
        return rcopy(ow_hbm.at[0, :, cols], ow.at[e], WOUT, o, e, (o, t))

    def hidden_copy(o):
        return rcopy(hid_out.at[o], hid_in.at[e], HIDDEN, o, e, (o, t))

    others(16, e, lambda o: wout_copy(o).start())
    ncs_ref[...] = jnp.concatenate([state[:, 1:, :], newest[:, None, :]], axis=1).astype(BF16)

    others(4, x, lambda o: rcopy(proj.at[0], proj_x.at[o], PROJ_X, o, o, (e, y * 4 + o)).wait_recv())
    total = proj[0].astype(F32)
    for d in range(1, 4):
        total = total + proj_x[lax.rem(x + d, 4)].astype(F32)
    proj[1] = total.astype(BF16)

    def proj_y_copy(o):
        return rcopy(proj.at[1], proj_y.at[y], PROJ_Y, o, y, (e, o * 4 + x))

    others(4, y, lambda o: proj_y_copy(o).start())
    others(16, e, lambda o: hidden_copy(o).start())
    for group in weights:
        for copy in group:
            copy.start()

    row = lax.broadcasted_iota(jnp.int32, (256, 256), 0)
    col = lax.broadcasted_iota(jnp.int32, (256, 256), 1)
    perm[...] = jnp.where(col == lax.rem(row, 16) * 16 + lax.div(row, 16), 1.0, 0.0).astype(BF16)
    hit = jnp.where(ids_ref[...] == expert, rw_ref[...], 0.0)
    wide = jnp.broadcast_to(jnp.sum(hit, axis=1, keepdims=True), (256, 128))
    high = wide.astype(BF16)
    rest = wide - high.astype(F32)
    mid = rest.astype(BF16)
    low = (rest - mid.astype(F32)).astype(BF16)
    wrow[...] = (
        jnp.dot(perm[...], high, preferred_element_type=F32)
        + jnp.dot(perm[...], mid, preferred_element_type=F32)
        + jnp.dot(perm[...], low, preferred_element_type=F32)
    )
    decay = -jnp.exp(alog_ref[...])
    gate_z = jax.nn.silu(z_ref[...].astype(F32))
    dtw_copy.wait()
    ssm_copy.wait()
    others(4, x, lambda o: proj_x_copy(o).wait_send())

    others(4, y, lambda o: rcopy(proj.at[1], proj_y.at[o], PROJ_Y, o, o, (e, o * 4 + x)).wait_recv())
    total = proj[1].astype(F32)
    for d in range(1, 4):
        total = total + proj_y[lax.rem(y + d, 4)].astype(F32)

    step_size = jax.nn.softplus(
        jnp.dot(total[:, 0:512].astype(BF16), dtw[...], preferred_element_type=F32) + dtb_ref[...]
    )
    maps = total[:, 512:640].T
    b_map, c_map = maps[0:16, :], maps[16:32, :]
    driven = step_size * inputs
    for r in range(16):
        new = jnp.exp(step_size[r : r + 1, :] * decay) * ssm[r] + driven[r : r + 1, :] * b_map[:, r : r + 1]
        nssm_ref[r] = new
        readout[r : r + 1, :] = jnp.sum(new * c_map[:, r : r + 1], axis=0, keepdims=True)
    mix[e] = ((readout[...] + skip_ref[...] * inputs) * gate_z).astype(BF16)

    def mix_copy(o):
        return rcopy(mix.at[e], mix.at[e], MIXED, o, e, (o, t))

    others(16, e, lambda o: mix_copy(o).start())
    others(4, y, lambda o: proj_y_copy(o).wait_send())
    others(16, e, lambda o: wout_copy(o).wait_send())
    others(16, e, lambda o: hidden_copy(o).wait_send())
    ow_copy.wait()
    others(16, e, lambda o: rcopy(ow.at[e], ow.at[o], WOUT, o, o, (o, t)).wait_recv())
    others(16, e, lambda o: rcopy(hid_out.at[o], hid_in.at[o], HIDDEN, o, o, (o, t)).wait_recv())
    others(16, e, lambda o: rcopy(mix.at[e], mix.at[o], MIXED, o, o, (o, t)).wait_recv())
    ordered = jnp.dot(perm[...], mix[...].reshape(256, 512), preferred_element_type=F32).astype(BF16)
    mixed = jnp.dot(ordered, ow[...].reshape(512, 256), preferred_element_type=F32)
    outb[...] = mixed.astype(BF16).reshape(16, 16, 256)

    def out_copy(o):
        return rcopy(outb.at[o], outr.at[t], OUTRED, o, t, (e, o))

    others(16, t, lambda o: out_copy(o).start())
    outr[t] = outb[t]
    others(16, e, lambda o: mix_copy(o).wait_send())
    others(16, t, lambda o: rcopy(outb.at[o], outr.at[o], OUTRED, o, o, (e, o)).wait_recv())
    res[e] = (jnp.sum(outr[...].astype(F32), axis=0) + hid_in[...].reshape(16, 256)).astype(BF16)

    def res_copy(o):
        return rcopy(res.at[e], res.at[e], RESID, o, e, (o, t))

    others(16, e, lambda o: res_copy(o).start())
    others(16, t, lambda o: out_copy(o).wait_send())
    others(16, e, lambda o: rcopy(res.at[e], res.at[o], RESID, o, o, (o, t)).wait_recv())
    squares = jnp.zeros((16, 256), F32)
    for b in range(16):
        piece = res[b].astype(F32)
        squares = squares + piece * piece
    scale = lax.rsqrt(jnp.sum(squares, axis=1, keepdims=True) * (1.0 / 4096) + 1e-5)
    for i in range(8):
        gain = gain_ref[:, pl.ds(pl.multiple_of(c * 2048 + i * 256, 256), 256)]
        value = (res[8 * c + i].astype(F32) * scale * gain).astype(BF16)
        xn[2 * c + i // 4, y, x, :, (i % 4) * 256 : (i % 4 + 1) * 256] = value

    q0, q1 = 2 * c, 2 * c + 1

    def rows1_x(o, frm):
        return rcopy(xn.at[q0, y, x], xn.at[q0, y, frm], ROWS1, o, frm, (e, y * 4 + o))

    def rows1_y(o, frm):
        return rcopy(xn.at[q1, y, x], xn.at[q1, frm, x], ROWS1, 4 + o, 4 + frm, (e, o * 4 + x))

    def rows2_y(o, frm):
        return rcopy(xn.at[q0, y], xn.at[q0, frm], ROWS2, o, frm, (e, o * 4 + x))

    def rows2_x(o, frm):
        return rcopy(xn.at[q1, :, x], xn.at[q1, :, frm], ROWS2, 4 + o, 4 + frm, (e, y * 4 + o))

    def rows3_0(q, o):
        return rcopy(xn.at[q, o], xn.at[q, o], ROWS3, o, o, (mate, t))

    def rows3_1(q, o):
        return rcopy(xn.at[q, :, o], xn.at[q, :, o], ROWS3, 4 + o, 4 + o, (mate, t))

    others(4, x, lambda o: rows1_x(o, x).start())
    others(4, y, lambda o: rows1_y(o, y).start())
    others(16, e, lambda o: res_copy(o).wait_send())
    mine = lax.broadcasted_iota(jnp.int32, (16, 256), 0) == e
    for b in range(16):
        resrow[b : b + 1, :] = jnp.sum(jnp.where(mine, res[b].astype(F32), 0.0), axis=0, keepdims=True)
    others(4, x, lambda o: rows1_x(o, o).wait_recv())
    others(4, y, lambda o: rows2_y(o, y).start())
    rows3_0(q0, y).start()
    others(4, y, lambda o: rows1_y(o, o).wait_recv())
    others(4, x, lambda o: rows2_x(o, x).start())
    rows3_1(q1, x).start()
    for group in weights:
        for copy in group:
            copy.wait()
    others(4, x, lambda o: rows1_x(o, x).wait_send())
    others(4, y, lambda o: rows1_y(o, y).wait_send())

    def forward(d, carry):
        oy, ox = lax.rem(y + d, 4), lax.rem(x + d, 4)
        rows2_y(oy, oy).wait_recv()
        rows3_0(q0, oy).start()
        rows2_x(ox, ox).wait_recv()
        rows3_1(q1, ox).start()
        return carry

    lax.fori_loop(1, 4, forward, 0)

    acc_g[...] = jnp.zeros((256, 384), F32)
    acc_u[...] = jnp.zeros((256, 384), F32)

    def project(q):
        rows = xn[q].reshape(256, 1024)
        acc_g[...] += jnp.dot(rows, wg[q], preferred_element_type=F32)
        acc_u[...] += jnp.dot(rows, wu[q], preferred_element_type=F32)

    def project_half(first):
        def step(s, carry):
            project(first + s)
            return carry
        lax.fori_loop(0, 2, step, 0)

    project_half(q0)
    p0 = 2 - 2 * c

    def mate_rows(o, carry):
        rows3_0(p0, o).wait_recv()
        rows3_1(p0 + 1, o).wait_recv()
        return carry

    lax.fori_loop(0, 4, mate_rows, 0)
    project_half(p0)
    weight = jnp.concatenate([wrow[...]] * 3, axis=1)
    actw[...] = (jax.nn.silu(acc_g[...]) * acc_u[...] * weight).astype(BF16)

    def pair_copy(s):
        return rcopy(osend.at[s], opair.at[s], PAIR, s, s, (mate, t))

    def down_mate(s, carry):
        value = jnp.dot(actw[...], wd[p0 + s], preferred_element_type=F32)
        osend[s] = value.astype(BF16).reshape(4, 4, 16, 1024)
        pair_copy(s).start()
        return carry

    lax.fori_loop(0, 2, down_mate, 0)

    def red1_x(o, frm):
        return rcopy(own.at[0, :, o], red1.at[0, frm], RED1, o, frm, (e, y * 4 + o))

    def red1_y(o, frm):
        return rcopy(own.at[1, o], red1.at[1, frm], RED1, 4 + o, 4 + frm, (e, o * 4 + x))

    def down_own(s):
        value = jnp.dot(actw[...], wd[q0 + s], preferred_element_type=F32)
        pair_copy(s).wait_recv()
        own[s] = (value + opair[s].astype(F32).reshape(256, 1024)).astype(BF16).reshape(4, 4, 16, 1024)

    down_own(0)
    others(4, x, lambda o: red1_x(o, x).start())
    down_own(1)
    others(4, y, lambda o: red1_y(o, y).start())

    others(4, y, lambda o: rows2_y(o, y).wait_send())
    others(4, x, lambda o: rows2_x(o, x).wait_send())

    def rows3_sent(o, carry):
        rows3_0(q0, o).wait_send()
        rows3_1(q1, o).wait_send()
        return carry

    lax.fori_loop(0, 4, rows3_sent, 0)
    pair_copy(0).wait_send()
    pair_copy(1).wait_send()

    def red2_y(o, frm):
        return rcopy(tsum.at[0, o], red2.at[0, frm], RED2, o, frm, (e, o * 4 + x))

    def red2_x(o, frm):
        return rcopy(tsum.at[1, o], red2.at[1, frm], RED2, 4 + o, 4 + frm, (e, y * 4 + o))

    others(4, x, lambda o: red1_x(o, o).wait_recv())
    value = own[0, :, x].astype(F32)
    for d in range(1, 4):
        value = value + red1[0, lax.rem(x + d, 4)].astype(F32)
    tsum[0] = value.astype(BF16)
    others(4, y, lambda o: red2_y(o, y).start())
    others(4, y, lambda o: red1_y(o, o).wait_recv())
    value = own[1, y].astype(F32)
    for d in range(1, 4):
        value = value + red1[1, lax.rem(y + d, 4)].astype(F32)
    tsum[1] = value.astype(BF16)
    others(4, x, lambda o: red2_x(o, x).start())
    others(4, x, lambda o: red1_x(o, x).wait_send())
    others(4, y, lambda o: red1_y(o, y).wait_send())

    others(4, y, lambda o: red2_y(o, o).wait_recv())
    first = tsum[0, y].astype(F32)
    for d in range(1, 4):
        first = first + red2[0, lax.rem(y + d, 4)].astype(F32)
    others(4, x, lambda o: red2_x(o, o).wait_recv())
    second = tsum[1, x].astype(F32)
    for d in range(1, 4):
        second = second + red2[1, lax.rem(x + d, 4)].astype(F32)

    for k in range(8):
        vrow[:, k, :] = first[:, 128 * k : 128 * (k + 1)]
        vrow[:, 8 + k, :] = second[:, 128 * k : 128 * (k + 1)]
    vsend[...] = vrow[...].astype(BF16)

    def final_copy(o):
        return rcopy(vsend.at[o], final_in.at[e], FINAL, o, e, (o, t))

    others(16, e, lambda o: final_copy(o).start())
    final_in[e] = vsend[e]
    others(4, y, lambda o: red2_y(o, y).wait_send())
    others(4, x, lambda o: red2_x(o, x).wait_send())
    others(16, e, lambda o: rcopy(vsend.at[o], final_in.at[o], FINAL, o, o, (o, t)).wait_recv())
    for half in range(2):
        value = final_in[half].astype(F32)
        for k in range(1, 8):
            value = value + final_in[2 * k + half].astype(F32)
        for k in range(16):
            m = 16 * half + k
            tail = resrow[m // 2 : m // 2 + 1, (m % 2) * 128 : (m % 2 + 1) * 128]
            out_ref[:, 128 * m : 128 * (m + 1)] = value[k : k + 1, :] + tail
    others(16, e, lambda o: final_copy(o).wait_send())


def local(
    hidden_in,
    x_stream,
    z_stream,
    conv_state,
    ssm_state,
    conv_weight,
    conv_bias,
    x_weight,
    dt_weight,
    dt_bias,
    a_log,
    skip_gain,
    out_weight,
    norm_gain,
    route_ids,
    route_weights,
    gate_proj,
    up_proj,
    down_proj,
):
    vmem = pl.BlockSpec(memory_space=pltpu.VMEM)
    hbm = pl.BlockSpec(memory_space=pl.ANY)
    row, new_conv_state, new_ssm_state = pl.pallas_call(
        layer_kernel,
        out_shape=(
            jax.ShapeDtypeStruct((1, 4096), F32),
            jax.ShapeDtypeStruct((16, 3, 512), BF16),
            jax.ShapeDtypeStruct((16, 16, 512), F32),
        ),
        in_specs=[vmem] * 13 + [hbm] * 6,
        out_specs=(vmem, vmem, vmem),
        scratch_shapes=[
            pltpu.VMEM((512, 512), BF16),
            pltpu.VMEM((16, 16, 512), F32),
            pltpu.VMEM((4, 1024, 384), BF16),
            pltpu.VMEM((4, 1024, 384), BF16),
            pltpu.VMEM((4, 384, 1024), BF16),
            pltpu.VMEM((16, 32, 256), BF16),
            pltpu.VMEM((2, 16, 640), BF16),
            pltpu.VMEM((4, 16, 640), BF16),
            pltpu.VMEM((4, 16, 640), BF16),
            pltpu.VMEM((16, 1, 256), F32),
            pltpu.VMEM((16, 1, 256), F32),
            pltpu.VMEM((16, 512), F32),
            pltpu.VMEM((16, 16, 512), BF16),
            pltpu.VMEM((16, 16, 256), BF16),
            pltpu.VMEM((16, 16, 256), BF16),
            pltpu.VMEM((16, 16, 256), BF16),
            pltpu.VMEM((16, 256), F32),
            pltpu.VMEM((4, 4, 4, 16, 1024), BF16),
            pltpu.VMEM((256, 384), F32),
            pltpu.VMEM((256, 384), F32),
            pltpu.VMEM((256, 384), BF16),
            pltpu.VMEM((256, 128), F32),
            pltpu.VMEM((256, 256), BF16),
            pltpu.VMEM((2, 4, 4, 16, 1024), BF16),
            pltpu.VMEM((2, 4, 4, 16, 1024), BF16),
            pltpu.VMEM((2, 4, 4, 16, 1024), BF16),
            pltpu.VMEM((2, 4, 4, 16, 1024), BF16),
            pltpu.VMEM((2, 4, 16, 1024), BF16),
            pltpu.VMEM((2, 4, 16, 1024), BF16),
            pltpu.VMEM((16, 16, 128), F32),
            pltpu.VMEM((16, 16, 128), BF16),
            pltpu.VMEM((16, 16, 128), BF16),
            pltpu.SemaphoreType.DMA((14, 16)),
            pltpu.SemaphoreType.DMA((14, 16)),
            pltpu.SemaphoreType.DMA((16,)),
        ],
        compiler_params=pltpu.CompilerParams(
            collective_id=0, has_side_effects=True, vmem_limit_bytes=48 * 1024 * 1024
        ),
        name="layer",
    )(
        x_stream, z_stream, conv_state, conv_weight, conv_bias[None], x_weight, dt_bias[None], a_log,
        skip_gain[None], norm_gain[None], route_ids, route_weights, hidden_in,
        dt_weight, ssm_state, out_weight, gate_proj, up_proj, down_proj,
    )
    return (row.astype(BF16), new_conv_state, new_ssm_state)


def solution(mesh):
    return jax.shard_map(
        local,
        mesh=mesh,
        in_specs=(
            P(("expert", "tensor"), None),
            P("expert", "tensor"),
            P("expert", "tensor"),
            P("expert", None, "tensor"),
            P("expert", None, "tensor"),
            P(None, "tensor"),
            P("tensor"),
            P("tensor", None),
            P(None, "tensor"),
            P("tensor"),
            P(None, "tensor"),
            P("tensor"),
            P("tensor", "expert", None),
            P(),
            P(),
            P(),
            P("expert", None, "tensor"),
            P("expert", None, "tensor"),
            P("expert", "tensor", None),
        ),
        out_specs=(
            P(("expert", "tensor"), None),
            P("expert", None, "tensor"),
            P("expert", None, "tensor"),
        ),
        check_vma=False,
    )
```

time: 796 us -> 95.9 us (0.12)
  waiting for transfers between devices: 636 us -> 0 us
  blocking collectives: 91.7 us -> 0 us
  Pallas kernels: 0 us -> 77.3 us
  matrix products: 14.5 us -> 0 us
  between operations: 14.6 us -> 0.68 us
  other arithmetic: 14.4 us -> 0.62 us
    unnamed x5 -> x0, waiting for transfers between devices: 521 us -> none
    all_gather x1 -> x0, waiting for transfers between devices: 116 us -> none  [local(): everyone = lax.all_gather(normed, ('expert', 'tensor'), axis=0, tiled=True)]
    pallas_call x0 -> x1, Pallas kernels: none -> 77.3 us  [local(): pl.pallas_call(layer_kernel, out_shape=(jax.ShapeDtypeStruct((1, 4096), F...]
    psum x1 -> x0, blocking collectives: 61.3 us -> none  [local(): lax.psum(partial_proj.astype(jnp.bfloat16), 'tensor').astype(jnp.float32)]
    all_to_all x1 -> x0, blocking collectives: 30.5 us -> none  [local(): lax.all_to_all(mixer_out, 'expert', split_axis=1, concat_axis=0, tiled=True)]
    dot_general x5 -> x0, matrix products: 14.5 us -> none  [the longest x1 5.94 us: expert_mlp(): return jnp.dot(active, w_down, preferred_element_type=jnp.float32)]
    gather x2 -> x0, local copies, waits for them, and re-layouts: 13.6 us -> none  [the longest x1 7.54 us: local(): gathered = result[jnp.clip(slot_place, 0, capacity - 1)]]
    unnamed x19 -> x32, local copies, waits for them, and re-layouts: 6.86 us -> 16.5 us
  transfers between devices with their start and end apart: 3 -> 0, of which waited for: 3 -> 0; matrix products, arithmetic and copies ran while one was open for 0% -> 0% of each run, Pallas kernels for 0% -> 0%
where the time goes in v1:
time: 95.9 us; the launch traced here: 95.1 us
  Pallas kernels  77.3 us (81%)
  local copies, waits for them, and re-layouts  16.5 us (17%)
    pallas_call x1, Pallas kernels, local(): pl.pallas_call(layer_kernel, out_shape=(jax.ShapeDtypeStruct((1, 4096), F...  77.3 us
    unnamed x32, local copies, waits for them, and re-layouts  16.5 us

profile of v1, /device:TPU:1, one launch (start us, length us, event | category | flops | bytes accessed | tf_op | source)
XLA Modules:
  0.0 95.1 jit_solution(344488206896264043)
XLA Ops:
  0.6 0.8 copy.22.cs_ref
  1.5 0.8 copy.24.ids_ref
  2.3 0.8 copy.25.rw_ref
  3.1 1.4 %copy.23.xw_ref = bf16[512,544]{1,0:T(8,128)(2,1)S(1)} copy(bf16[512,544]{0,1:T(8,128)(2,1)} %param.26) | data formatting | bytes 1114112 | tf_op args[7]
  4.5 0.0 copy-start
  4.5 1.9 %copy-done = bf16[1,4096,384]{2,1,0:T(8,128)(2,1)S(1)} copy-done((bf16[1,4096,384]{2,1,0:T(8,128)(2,1)S(1)}, bf16[1,4096,384]{2,1,0:T(8,128)(2,1)}, u32[]{:S(2)}) %copy-start) | copy-done | bytes 3145752
  6.4 0.0 copy-start.1
  6.4 1.0 %copy-done.1 = bf16[512,512]{1,0:T(8,128)(2,1)S(1)} copy-done((bf16[512,512]{1,0:T(8,128)(2,1)S(1)}, bf16[512,512]{1,0:T(8,128)(2,1)}, u32[]{:S(2)}) %copy-start.1) | copy-done | bytes 524312
  7.4 0.0 copy-start.2
  7.4 1.0 %copy-done.2 = f32[16,16,512]{2,1,0:T(8,128)S(1)} copy-done((f32[16,16,512]{2,1,0:T(8,128)S(1)}, f32[16,16,512]{2,1,0:T(8,128)}, u32[]{:S(2)}) %copy-start.2) | copy-done | bytes 524312
  8.4 0.0 copy-start.3
  8.5 0.9 copy-done.3
  9.4 0.0 copy-start.4
  9.4 0.8 copy-done.4
  10.2 0.0 copy-start.5
  10.2 0.7 copy-done.5
  10.9 0.0 copy-start.6
  10.9 0.7 copy-done.6
  11.6 0.0 copy-start.7
  11.6 0.7 copy-done.7
  12.3 0.0 copy-start.8
  12.3 0.7 copy-done.8
  13.0 0.0 copy-start.9
  13.0 0.7 copy-done.9
  13.7 0.0 copy-start.10
  13.7 0.7 copy-done.10
  14.4 0.7 copy-done.11
  15.1 0.7 copy-done.12
  15.8 77.3 %layer.1 = (f32[1,4096]{1,0:T(1,128)S(1)}, bf16[16,3,512]{2,1,0:T(4,128)(2,1)S(1)}, f32[16,16,512]{2,1,0:T(8,128)S(1)}) custom-call(bf16[16,512]{1,0:T(8,128)(2,1)S(1)} %copy-done.5, bf16[16,512]{1,0:T(8,128)(2,1)S(1)} %copy-done.6, bf16[16,3,512]{2,1,0:T(4,128)(2,1)S(1)} %copy.22.cs_ref, bf16[4,512]{1,0:T(4,128)(2,1)S(1)} %copy-done.9, ...), custom_call_target="tpu_custom_call" | custom-call | tf_op jit(solution)/shard_map/layer/pallas_call | solution.py:381
  93.1 0.6 convert_element_type.3
  93.7 0.6 copy.26
  94.3 0.8 copy.28
  (2 shorter events, 0.0 us)
Async XLA Ops:
  4.5 1.9 %copy-start = (bf16[1,4096,384]{2,1,0:T(8,128)(2,1)S(1)}, bf16[1,4096,384]{2,1,0:T(8,128)(2,1)}, u32[]{:S(2)}) copy-start(bf16[1,4096,384]{2,1,0:T(8,128)(2,1)} %gate_hbm.1) | copy-start | bytes 9437188
  6.4 1.0 %copy-start.1 = (bf16[512,512]{1,0:T(8,128)(2,1)S(1)}, bf16[512,512]{1,0:T(8,128)(2,1)}, u32[]{:S(2)}) copy-start(bf16[512,512]{1,0:T(8,128)(2,1)} %dtw_hbm.1) | copy-start | bytes 1572868
  7.4 1.0 %copy-start.2 = (f32[16,16,512]{2,1,0:T(8,128)S(1)}, f32[16,16,512]{2,1,0:T(8,128)}, u32[]{:S(2)}) copy-start(f32[16,16,512]{2,1,0:T(8,128)} %ssm_hbm.1) | copy-start | bytes 1572868
  8.4 0.9 copy-start.3
  9.4 0.8 copy-start.4
  10.2 0.7 copy-start.5
  10.9 0.7 copy-start.6
  11.6 0.7 copy-start.7
  12.3 0.7 copy-start.8
  13.0 0.7 copy-start.9
  13.7 0.7 copy-start.10
  14.4 0.7 copy-start.11
  15.1 0.7 copy-start.12

commit v2 on v1

v2 whole, which is shorter than its diff:
```python
import jax
import jax.numpy as jnp
from jax import lax
from jax.experimental import pallas as pl
from jax.experimental.pallas import tpu as pltpu
from jax.sharding import PartitionSpec as P

F32 = jnp.float32
BF16 = jnp.bfloat16
MESH = pl.DeviceIdType.MESH

(
    PROJ, WOUT_M, WOUT, HID_M, HID, DOWN_M, MIX, MIX_M, OUTRED, RESID, STAT, SCALE,
    ROWS1, ROWS2, ROWS3, ACT, RED1, RED2, FINAL, FINAL_M,
) = range(20)


def layer_kernel(
    x_hbm, z_hbm, cs_hbm, cw_hbm, cb_hbm, xw_hbm, dtb_hbm, alog_hbm, skip_hbm, gain_hbm, ids_hbm, rw_hbm, hid_hbm,
    dtw_hbm, ssm_hbm, ow_hbm, gate_hbm, up_hbm, down_hbm,
    out_ref, ncs_hbm, nssm_hbm,
    ncs_ref, nssm_ref, x_ref, z_ref, cs_ref, cw_ref, cb_ref, xw_ref, dtb_ref, alog_ref, skip_ref, gain_ref, ids_ref, rw_ref, hid_ref,
    dtw, ssm, wg, wu, wd, wd_mate, owh, ow,
    proj, proj_in, hid_out, hidh, hid_in, readout, mix, outb, outr, res, stat, scales, resrow, xn, acc_g, acc_u,
    actw, act_mate, wrow, perm, own, red1, tsum, red2, vrow, vsend, final_in, fbuf, fmate,
    ssem, rsem, lsem,
):
    e = lax.axis_index("expert")
    t = lax.axis_index("tensor")
    y, x = lax.div(t, 4), lax.rem(t, 4)
    z, c = lax.div(e, 2), lax.rem(e, 2)
    m = 1 - c
    mate = 2 * z + m
    q0, q1 = 2 * c, 2 * c + 1
    p0 = 2 * m

    def rcopy(src, dst, phase, to, frm, device):
        return pltpu.make_async_remote_copy(
            src_ref=src, dst_ref=dst, send_sem=ssem.at[phase, to], recv_sem=rsem.at[phase, frm],
            device_id=device, device_id_type=MESH,
        )

    def others(n, me, body):
        def step(d, carry):
            body(lax.rem(me + d, n))
            return carry
        lax.fori_loop(1, n, step, 0)

    def at_z(o):
        return (2 * o + c, t)

    def at_x(o):
        return (e, y * 4 + o)

    def at_y(o):
        return (e, o * 4 + x)

    def half(which):
        return pl.ds(pl.multiple_of(which * 2048, 2048), 2048)

    def lcopy(src, dst, i):
        return pltpu.make_async_copy(src, dst, lsem.at[i])

    early = [
        lcopy(src, dst, i) for i, (src, dst) in enumerate((
            (x_hbm, x_ref), (cs_hbm, cs_ref), (cw_hbm, cw_ref), (cb_hbm, cb_ref), (xw_hbm, xw_ref),
        ))
    ]
    later = [
        lcopy(src, dst, 5 + i) for i, (src, dst) in enumerate((
            (hid_hbm, hid_ref), (dtw_hbm, dtw), (ssm_hbm, ssm), (ids_hbm, ids_ref), (rw_hbm, rw_ref),
            (z_hbm, z_ref), (dtb_hbm, dtb_ref), (alog_hbm, alog_ref), (skip_hbm, skip_ref), (gain_hbm, gain_ref),
        ))
    ]
    weights = []
    for q in range(4):
        weights.append(lcopy(gate_hbm.at[0, pl.ds(q * 1024, 1024), :], wg.at[q], 16 + q))
        weights.append(lcopy(up_hbm.at[0, pl.ds(q * 1024, 1024), :], wu.at[q], 20 + q))

    def down_cols(which, s):
        return down_hbm.at[0, :, pl.ds(pl.multiple_of(which * 2048 + s * 1024, 1024), 1024)]

    for s in range(2):
        weights.append(lcopy(down_cols(c, s), wd.at[s], 24 + s))
    own_weight = lcopy(ow_hbm.at[0, :, half(c)], owh.at[c], 15)
    for copy in early:
        copy.start()
    own_weight.start()

    def greet(device):
        pl.semaphore_signal(bar, inc=1, device_id=device, device_id_type=MESH)

    bar = pltpu.get_barrier_semaphore()
    others(16, t, lambda o: greet((e, o)))
    others(8, z, lambda o: greet(at_z(o)))
    greet((mate, t))

    for copy in early:
        copy.wait()
    state = cs_ref[...].astype(F32)
    taps = cw_ref[...].astype(F32)
    newest = x_ref[...].astype(F32)
    window = [state[0], state[1], state[2], newest]
    conv_sum = sum(window[k] * taps[k : k + 1, :] for k in range(4)) + cb_ref[...]
    conv_out = jax.nn.silu(conv_sum).astype(BF16)
    inputs = conv_out.astype(F32)
    part = lax.dot_general(
        conv_out, xw_ref[...], (((1,), (1,)), ((), ())), preferred_element_type=F32
    )
    proj[...] = jnp.zeros((16, 640), BF16)
    proj[:, 0:544] = part.astype(BF16)

    pl.semaphore_wait(bar, 23)

    def wout_copy(o):
        cols = pl.ds(pl.multiple_of(o * 256, 256), 256)
        return rcopy(owh.at[:, :, cols], ow.at[z], WOUT, o, z, at_z(o))

    def wout_from(o):
        return rcopy(ow.at[o], ow.at[o], WOUT, o, o, at_z(o))

    def proj_copy(o):
        return rcopy(proj, proj_in.at[t], PROJ, o, t, (e, o))

    wout_mate = rcopy(ow_hbm.at[0, :, half(m)], owh.at[c], WOUT_M, 0, 0, (mate, t))
    wout_from_mate = rcopy(ow_hbm.at[0, :, half(m)], owh.at[m], WOUT_M, 0, 0, (mate, t))
    wout_mate.start()
    others(16, t, lambda o: proj_copy(o).start())
    proj_in[t] = proj[...]
    wout_from_mate.wait_recv()
    own_weight.wait()
    others(8, z, lambda o: wout_copy(o).start())

    hid_mate = rcopy(hid_out.at[pl.ds(8 * m, 8)], hidh.at[:, c], HID_M, 0, 0, (mate, t))
    hid_from_mate = rcopy(hid_out.at[pl.ds(8 * m, 8)], hidh.at[:, m], HID_M, 0, 0, (mate, t))

    def down_mate(s):
        return rcopy(down_cols(m, s), wd_mate.at[s], DOWN_M, s, s, (mate, t))

    for copy in later:
        copy.start()
    for copy in later:
        copy.wait()
    hidden = hid_ref[...].astype(F32)
    for k in range(16):
        hid_out[k] = hidden[:, 256 * k : 256 * (k + 1)]
    hid_mate.start()
    hidh[:, c] = hid_out[pl.ds(8 * c, 8)]
    ncs_ref[0] = cs_ref[1]
    ncs_ref[1] = cs_ref[2]
    ncs_ref[2] = x_ref[...]
    ncs_copy = lcopy(ncs_ref, ncs_hbm, 26)
    ncs_copy.start()

    ow[z] = owh[:, :, pl.ds(pl.multiple_of(z * 256, 256), 256)]

    def hid_copy(o):
        return rcopy(hidh.at[o], hid_in.at[z], HID, o, z, at_z(o))

    def hid_from(o):
        return rcopy(hidh.at[o], hid_in.at[o], HID, o, o, at_z(o))

    row = lax.broadcasted_iota(jnp.int32, (256, 256), 0)
    col = lax.broadcasted_iota(jnp.int32, (256, 256), 1)
    chosen = col == lax.rem(row, 16) * 16 + lax.div(row, 16)
    perm[...] = jnp.where(chosen, 1.0, 0.0).astype(BF16)
    hit = jnp.sum(jnp.where(ids_ref[...] == z, rw_ref[...], 0.0), axis=0, keepdims=True)
    picked = jnp.sum(jnp.where(chosen, hit, 0.0), axis=1, keepdims=True)
    wrow[...] = jnp.broadcast_to(picked, (256, 128))
    decay = -jnp.exp(alog_ref[...])
    gate_z = jax.nn.silu(z_ref[...].astype(F32))
    wout_mate.wait_send()
    hid_mate.wait_send()

    others(16, t, lambda o: rcopy(proj, proj_in.at[o], PROJ, o, o, (e, o)).wait_recv())
    total = jnp.sum(proj_in[...].astype(F32), axis=0)

    step_size = jax.nn.softplus(
        jnp.dot(total[:, 0:512].astype(BF16), dtw[...], preferred_element_type=F32) + dtb_ref[...]
    )
    maps = total[:, 512:640].T
    b_map, c_map = maps[0:16, :], maps[16:32, :]
    driven = step_size * inputs
    for r in range(16):
        new = jnp.exp(step_size[r : r + 1, :] * decay) * ssm[r] + driven[r : r + 1, :] * b_map[:, r : r + 1]
        nssm_ref[r] = new
        readout[r : r + 1, :] = jnp.sum(new * c_map[:, r : r + 1], axis=0, keepdims=True)
    nssm_copy = lcopy(nssm_ref, nssm_hbm, 27)
    nssm_copy.start()
    mix[e] = ((readout[...] + skip_ref[...] * inputs) * gate_z).astype(BF16)

    def mix_copy(o):
        return rcopy(mix.at[e], mix.at[e], MIX, o, z, at_z(o))

    def mix_from(o):
        return rcopy(mix.at[2 * o + c], mix.at[2 * o + c], MIX, o, o, at_z(o))

    def mix_to_mate(o):
        return rcopy(mix.at[2 * o + c], mix.at[2 * o + c], MIX_M, o, o, (mate, t))

    def mix_from_mate(o):
        return rcopy(mix.at[2 * o + m], mix.at[2 * o + m], MIX_M, o, o, (mate, t))

    others(8, z, lambda o: mix_copy(o).start())
    mix_to_mate(z).start()
    hid_from_mate.wait_recv()
    others(8, z, lambda o: hid_copy(o).start())
    hid_in[z] = hidh[z]
    for copy in weights:
        copy.start()
    others(8, z, lambda o: wout_from(o).wait_recv())

    def mix_pass(o):
        mix_from(o).wait_recv()
        mix_to_mate(o).start()

    others(8, z, mix_pass)
    mix_from_mate(z).wait_recv()
    others(8, z, lambda o: mix_from_mate(o).wait_recv())
    ordered = jnp.dot(perm[...], mix[...].reshape(256, 512), preferred_element_type=F32).astype(BF16)
    mixed = jnp.dot(ordered, ow[...].reshape(512, 256), preferred_element_type=F32)
    outb[...] = mixed.astype(BF16).reshape(16, 16, 256)

    def out_copy(o):
        return rcopy(outb.at[o], outr.at[t], OUTRED, o, t, (e, o))

    others(16, t, lambda o: out_copy(o).start())
    outr[t] = outb[t]
    down_mate(0).start()
    down_mate(1).start()
    others(16, t, lambda o: proj_copy(o).wait_send())
    others(8, z, lambda o: wout_copy(o).wait_send())
    others(8, z, lambda o: hid_copy(o).wait_send())
    others(8, z, lambda o: hid_from(o).wait_recv())
    others(8, z, lambda o: mix_copy(o).wait_send())
    mix_to_mate(z).wait_send()
    others(8, z, lambda o: mix_to_mate(o).wait_send())
    others(16, t, lambda o: rcopy(outb.at[o], outr.at[o], OUTRED, o, o, (e, o)).wait_recv())
    res[z] = (jnp.sum(outr[...].astype(F32), axis=0) + hid_in[...].reshape(16, 256)).astype(BF16)

    def res_copy(o):
        return rcopy(res.at[z], res.at[z], RESID, o, z, at_z(o))

    others(8, z, lambda o: res_copy(o).start())
    others(16, t, lambda o: out_copy(o).wait_send())
    others(8, z, lambda o: rcopy(res.at[o], res.at[o], RESID, o, o, at_z(o)).wait_recv())
    for b in range(8):
        gain = gain_ref[:, pl.ds(pl.multiple_of(c * 2048 + b * 256, 256), 256)]
        value = (res[b].astype(F32) * gain).astype(BF16)
        xn[2 * c + b // 4, y, x, :, (b % 4) * 256 : (b % 4 + 1) * 256] = value

    def rows1_x(o, frm):
        return rcopy(xn.at[q0, y, x], xn.at[q0, y, frm], ROWS1, o, frm, at_x(o))

    def rows1_y(o, frm):
        return rcopy(xn.at[q1, y, x], xn.at[q1, frm, x], ROWS1, 4 + o, 4 + frm, at_y(o))

    def rows2_y(o, frm):
        return rcopy(xn.at[q0, y], xn.at[q0, frm], ROWS2, o, frm, at_y(o))

    def rows2_x(o, frm):
        return rcopy(xn.at[q1, :, x], xn.at[q1, :, frm], ROWS2, 4 + o, 4 + frm, at_x(o))

    def rows3_0(q, o):
        return rcopy(xn.at[q, o], xn.at[q, o], ROWS3, o, o, (mate, t))

    def rows3_1(q, o):
        return rcopy(xn.at[q, :, o], xn.at[q, :, o], ROWS3, 4 + o, 4 + o, (mate, t))

    others(4, x, lambda o: rows1_x(o, x).start())
    others(4, y, lambda o: rows1_y(o, y).start())
    squares = jnp.zeros((16, 256), F32)
    for b in range(8):
        piece = res[b].astype(F32)
        squares = squares + piece * piece
    sums = jnp.broadcast_to(jnp.sum(squares, axis=1, keepdims=True), (16, 128)).T
    stat[0] = jnp.zeros((1, 128), F32)
    stat[0, :, 0:16] = sums[0:1, :]
    stat_copy = rcopy(stat.at[0], stat.at[1], STAT, 0, 0, (mate, t))
    stat_copy.start()
    others(8, z, lambda o: res_copy(o).wait_send())
    stat_copy.wait()
    scales[t] = lax.rsqrt((stat[0] + stat[1]) * (1.0 / 4096) + 1e-5)

    def scale_copy(o):
        return rcopy(scales.at[t], scales.at[t], SCALE, o, t, (e, o))

    others(16, t, lambda o: scale_copy(o).start())
    place = lax.broadcasted_iota(jnp.int32, (16, 256), 0)
    for k in range(2):
        mine = place == 2 * z + k
        for b in range(8):
            resrow[k, b : b + 1, :] = jnp.sum(jnp.where(mine, res[b].astype(F32), 0.0), axis=0, keepdims=True)
    others(4, x, lambda o: rows1_x(o, o).wait_recv())
    others(4, y, lambda o: rows2_y(o, y).start())
    rows3_0(q0, y).start()
    others(4, y, lambda o: rows1_y(o, o).wait_recv())
    others(4, x, lambda o: rows2_x(o, x).start())
    rows3_1(q1, x).start()
    for copy in weights:
        copy.wait()
    for s in range(2):
        down_mate(s).wait()
    others(4, x, lambda o: rows1_x(o, x).wait_send())
    others(4, y, lambda o: rows1_y(o, y).wait_send())

    others(16, t, lambda o: rcopy(scales.at[o], scales.at[o], SCALE, o, o, (e, o)).wait_recv())
    lane = lax.broadcasted_iota(jnp.int32, (16, 16, 128), 2)
    slot = lax.broadcasted_iota(jnp.int32, (16, 16, 128), 1)
    picked = jnp.where(lane == slot, jnp.broadcast_to(scales[...], (16, 16, 128)), 0.0).reshape(256, 128)
    scale = jnp.broadcast_to(jnp.sum(picked, axis=1, keepdims=True), (256, 384))

    def forward(d, carry):
        oy, ox = lax.rem(y + d, 4), lax.rem(x + d, 4)
        rows2_y(oy, oy).wait_recv()
        rows3_0(q0, oy).start()
        rows2_x(ox, ox).wait_recv()
        rows3_1(q1, ox).start()
        return carry

    lax.fori_loop(1, 4, forward, 0)

    acc_g[...] = jnp.zeros((256, 384), F32)
    acc_u[...] = jnp.zeros((256, 384), F32)

    def project(q):
        rows = xn[q].reshape(256, 1024)
        acc_g[...] += jnp.dot(rows, wg[q], preferred_element_type=F32)
        acc_u[...] += jnp.dot(rows, wu[q], preferred_element_type=F32)

    def project_half(first):
        def step(s, carry):
            project(first + s)
            return carry
        lax.fori_loop(0, 2, step, 0)

    project_half(q0)

    def mate_rows(o, carry):
        rows3_0(p0, o).wait_recv()
        rows3_1(p0 + 1, o).wait_recv()
        return carry

    lax.fori_loop(0, 4, mate_rows, 0)
    project_half(p0)
    weight = jnp.concatenate([wrow[...]] * 3, axis=1)
    actw[...] = (jax.nn.silu(acc_g[...] * scale) * (acc_u[...] * scale) * weight).astype(BF16)

    act_copy = rcopy(actw, act_mate, ACT, 0, 0, (mate, t))
    act_copy.start()

    def red1_x(o, frm):
        return rcopy(own.at[0, :, o], red1.at[0, frm], RED1, o, frm, at_x(o))

    def red1_y(o, frm):
        return rcopy(own.at[1, o], red1.at[1, frm], RED1, 4 + o, 4 + frm, at_y(o))

    value = jnp.dot(actw[...], wd[0], preferred_element_type=F32)
    act_copy.wait()
    value = value + jnp.dot(act_mate[...], wd_mate[0], preferred_element_type=F32)
    own[0] = value.astype(BF16).reshape(4, 4, 16, 1024)
    others(4, x, lambda o: red1_x(o, x).start())
    value = jnp.dot(actw[...], wd[1], preferred_element_type=F32)
    value = value + jnp.dot(act_mate[...], wd_mate[1], preferred_element_type=F32)
    own[1] = value.astype(BF16).reshape(4, 4, 16, 1024)
    others(4, y, lambda o: red1_y(o, y).start())

    others(16, t, lambda o: scale_copy(o).wait_send())
    others(4, y, lambda o: rows2_y(o, y).wait_send())
    others(4, x, lambda o: rows2_x(o, x).wait_send())

    def rows3_sent(o, carry):
        rows3_0(q0, o).wait_send()
        rows3_1(q1, o).wait_send()
        return carry

    lax.fori_loop(0, 4, rows3_sent, 0)

    def red2_y(o, frm):
        return rcopy(tsum.at[0, o], red2.at[0, frm], RED2, o, frm, at_y(o))

    def red2_x(o, frm):
        return rcopy(tsum.at[1, o], red2.at[1, frm], RED2, 4 + o, 4 + frm, at_x(o))

    others(4, x, lambda o: red1_x(o, o).wait_recv())
    value = own[0, :, x].astype(F32)
    for d in range(1, 4):
        value = value + red1[0, lax.rem(x + d, 4)].astype(F32)
    tsum[0] = value.astype(BF16)
    others(4, y, lambda o: red2_y(o, y).start())
    others(4, y, lambda o: red1_y(o, o).wait_recv())
    value = own[1, y].astype(F32)
    for d in range(1, 4):
        value = value + red1[1, lax.rem(y + d, 4)].astype(F32)
    tsum[1] = value.astype(BF16)
    others(4, x, lambda o: red2_x(o, x).start())
    others(4, x, lambda o: red1_x(o, x).wait_send())
    others(4, y, lambda o: red1_y(o, y).wait_send())

    others(4, y, lambda o: red2_y(o, o).wait_recv())
    first = tsum[0, y].astype(F32)
    for d in range(1, 4):
        first = first + red2[0, lax.rem(y + d, 4)].astype(F32)
    others(4, x, lambda o: red2_x(o, o).wait_recv())
    second = tsum[1, x].astype(F32)
    for d in range(1, 4):
        second = second + red2[1, lax.rem(x + d, 4)].astype(F32)

    for k in range(8):
        vrow[:, k, :] = first[:, 128 * k : 128 * (k + 1)]
        vrow[:, 8 + k, :] = second[:, 128 * k : 128 * (k + 1)]
    vsend[...] = vrow[...].astype(BF16).reshape(8, 2, 16, 128)

    def final_copy(o):
        return rcopy(vsend.at[o], final_in.at[z], FINAL, o, z, at_z(o))

    others(8, z, lambda o: final_copy(o).start())
    final_in[z] = vsend[z]
    others(4, y, lambda o: red2_y(o, y).wait_send())
    others(4, x, lambda o: red2_x(o, x).wait_send())
    others(8, z, lambda o: rcopy(vsend.at[o], final_in.at[o], FINAL, o, o, at_z(o)).wait_recv())
    rows = jnp.sum(final_in[...].astype(F32), axis=0)
    for k in range(2):
        for b in range(16):
            tail = resrow[k, b // 2 : b // 2 + 1, (b % 2) * 128 : (b % 2 + 1) * 128]
            fbuf[k, :, 128 * b : 128 * (b + 1)] = rows[k, b : b + 1, :] + tail
    final_mate = rcopy(fbuf.at[m], fmate, FINAL_M, 0, 0, (mate, t))
    final_mate.start()
    out_ref[:, half(c)] = fbuf[c]
    others(8, z, lambda o: final_copy(o).wait_send())
    final_mate.wait()
    ncs_copy.wait()
    nssm_copy.wait()
    out_ref[:, half(m)] = fmate[...]


def finish_kernel(row, ncs, nssm, row_out, ncs_out, nssm_out, row_in, ncs_in, nssm_in, sem):
    copies = [
        pltpu.make_async_copy(src, dst, sem.at[k])
        for k, (src, dst) in enumerate((
            (nssm, nssm_in), (ncs, ncs_in), (row, row_in), (nssm_in, nssm_out), (ncs_in, ncs_out),
        ))
    ]
    for k in range(3):
        copies[k].start()
    for k in range(2):
        copies[k].wait()
        copies[3 + k].start()
    copies[2].wait()
    row_out[...] = row_in[...].astype(BF16)
    copies[3].wait()
    copies[4].wait()


def local(
    hidden_in,
    x_stream,
    z_stream,
    conv_state,
    ssm_state,
    conv_weight,
    conv_bias,
    x_weight,
    dt_weight,
    dt_bias,
    a_log,
    skip_gain,
    out_weight,
    norm_gain,
    route_ids,
    route_weights,
    gate_proj,
    up_proj,
    down_proj,
):
    vmem = pl.BlockSpec(memory_space=pltpu.VMEM)
    hbm = pl.BlockSpec(memory_space=pltpu.HBM)
    row, new_conv_state, new_ssm_state = pl.pallas_call(
        layer_kernel,
        out_shape=(
            jax.ShapeDtypeStruct((1, 4096), F32),
            jax.ShapeDtypeStruct((3, 16, 512), BF16),
            jax.ShapeDtypeStruct((16, 16, 512), F32),
        ),
        in_specs=[hbm] * 19,
        out_specs=(vmem, hbm, hbm),
        scratch_shapes=[
            pltpu.VMEM((3, 16, 512), BF16),
            pltpu.VMEM((16, 16, 512), F32),
            pltpu.VMEM((16, 512), BF16),
            pltpu.VMEM((16, 512), BF16),
            pltpu.VMEM((3, 16, 512), BF16),
            pltpu.VMEM((4, 512), BF16),
            pltpu.VMEM((1, 512), F32),
            pltpu.VMEM((544, 512), BF16),
            pltpu.VMEM((1, 512), F32),
            pltpu.VMEM((16, 512), F32),
            pltpu.VMEM((1, 512), F32),
            pltpu.VMEM((1, 4096), F32),
            pltpu.VMEM((2, 256), jnp.int32),
            pltpu.VMEM((2, 256), F32),
            pltpu.VMEM((1, 4096), BF16),
            pltpu.VMEM((512, 512), BF16),
            pltpu.VMEM((16, 16, 512), F32),
            pltpu.VMEM((4, 1024, 384), BF16),
            pltpu.VMEM((4, 1024, 384), BF16),
            pltpu.VMEM((2, 384, 1024), BF16),
            pltpu.VMEM((2, 384, 1024), BF16),
            pltpu.VMEM((2, 32, 2048), BF16),
            pltpu.VMEM((8, 2, 32, 256), BF16),
            pltpu.VMEM((16, 640), BF16),
            pltpu.VMEM((16, 16, 640), BF16),
            pltpu.VMEM((16, 1, 256), F32),
            pltpu.VMEM((8, 2, 1, 256), F32),
            pltpu.VMEM((8, 2, 1, 256), F32),
            pltpu.VMEM((16, 512), F32),
            pltpu.VMEM((16, 16, 512), BF16),
            pltpu.VMEM((16, 16, 256), BF16),
            pltpu.VMEM((16, 16, 256), BF16),
            pltpu.VMEM((8, 16, 256), BF16),
            pltpu.VMEM((2, 1, 128), F32),
            pltpu.VMEM((16, 1, 128), F32),
            pltpu.VMEM((2, 8, 256), F32),
            pltpu.VMEM((4, 4, 4, 16, 1024), BF16),
            pltpu.VMEM((256, 384), F32),
            pltpu.VMEM((256, 384), F32),
            pltpu.VMEM((256, 384), BF16),
            pltpu.VMEM((256, 384), BF16),
            pltpu.VMEM((256, 128), F32),
            pltpu.VMEM((256, 256), BF16),
            pltpu.VMEM((2, 4, 4, 16, 1024), BF16),
            pltpu.VMEM((2, 4, 4, 16, 1024), BF16),
            pltpu.VMEM((2, 4, 16, 1024), BF16),
            pltpu.VMEM((2, 4, 16, 1024), BF16),
            pltpu.VMEM((16, 16, 128), F32),
            pltpu.VMEM((8, 2, 16, 128), BF16),
            pltpu.VMEM((8, 2, 16, 128), BF16),
            pltpu.VMEM((2, 1, 2048), F32),
            pltpu.VMEM((1, 2048), F32),
            pltpu.SemaphoreType.DMA((20, 16)),
            pltpu.SemaphoreType.DMA((20, 16)),
            pltpu.SemaphoreType.DMA((28,)),
        ],
        compiler_params=pltpu.CompilerParams(
            collective_id=0, has_side_effects=True, vmem_limit_bytes=58 * 1024 * 1024
        ),
        name="layer",
    )(
        x_stream, z_stream, conv_state.transpose(1, 0, 2), conv_weight, conv_bias[None], x_weight.T, dt_bias[None],
        a_log, skip_gain[None], norm_gain[None], route_ids.T, route_weights.T, hidden_in,
        dt_weight, ssm_state, out_weight, gate_proj, up_proj, down_proj,
    )
    row, new_conv_state, new_ssm_state = pl.pallas_call(
        finish_kernel,
        out_shape=(
            jax.ShapeDtypeStruct((1, 4096), BF16),
            jax.ShapeDtypeStruct((3, 16, 512), BF16),
            jax.ShapeDtypeStruct((16, 16, 512), F32),
        ),
        in_specs=[hbm] * 3,
        out_specs=(vmem, hbm, hbm),
        scratch_shapes=[
            pltpu.VMEM((1, 4096), F32),
            pltpu.VMEM((3, 16, 512), BF16),
            pltpu.VMEM((16, 16, 512), F32),
            pltpu.SemaphoreType.DMA((5,)),
        ],
        compiler_params=pltpu.CompilerParams(vmem_limit_bytes=58 * 1024 * 1024),
        name="finish",
    )(row, new_conv_state, new_ssm_state)
    return (row, new_conv_state.transpose(1, 0, 2), new_ssm_state)


def solution(mesh):
    return jax.shard_map(
        local,
        mesh=mesh,
        in_specs=(
            P(("expert", "tensor"), None),
            P("expert", "tensor"),
            P("expert", "tensor"),
            P("expert", None, "tensor"),
            P("expert", None, "tensor"),
            P(None, "tensor"),
            P("tensor"),
            P("tensor", None),
            P(None, "tensor"),
            P("tensor"),
            P(None, "tensor"),
            P("tensor"),
            P("tensor", "expert", None),
            P(),
            P(),
            P(),
            P("expert", None, "tensor"),
            P("expert", None, "tensor"),
            P("expert", "tensor", None),
        ),
        out_specs=(
            P(("expert", "tensor"), None),
            P("expert", None, "tensor"),
            P("expert", None, "tensor"),
        ),
        check_vma=False,
    )
```

time: 95.9 us -> 81.6 us (0.85)
  local copies, waits for them, and re-layouts: 16.5 us -> 0 us
  Pallas kernels: 77.3 us -> 80.7 us
    unnamed x32 -> x0, local copies, waits for them, and re-layouts: 16.5 us -> none
    pallas_call x0 -> x1, Pallas kernels: none -> 2.48 us  [local(): pl.pallas_call(finish_kernel, out_shape=(jax.ShapeDtypeStruct((1, 4096),...]
where the time goes in v2:
time: 81.6 us; the launch traced here: 81.3 us
  Pallas kernels  80.7 us (99%)
    pallas_call x1, Pallas kernels, local(): pl.pallas_call(layer_kernel, out_shape=(jax.ShapeDtypeStruct((1, 4096), F...  78.2 us
    pallas_call x1, Pallas kernels, local(): pl.pallas_call(finish_kernel, out_shape=(jax.ShapeDtypeStruct((1, 4096),...  2.48 us

profile of v2, /device:TPU:1, one launch (start us, length us, event | category | flops | bytes accessed | tf_op | source)
XLA Modules:
  0.0 81.3 jit_solution(5517148449855050420)
XLA Ops:
  0.6 78.2 %layer.1 = (f32[1,4096]{1,0:T(1,128)}, bf16[3,16,512]{2,1,0:T(8,128)(2,1)}, f32[16,16,512]{2,1,0:T(8,128)}) custom-call(bf16[16,512]{1,0:T(8,128)(2,1)} %x_hbm.1, bf16[16,512]{1,0:T(8,128)(2,1)} %z_hbm.1, bf16[3,16,512]{2,1,0:T(8,128)(2,1)} %bitcast.10, bf16[4,512]{1,0:T(4,128)(2,1)} %cw_hbm.1, f32[1,512]{1,0:T(1,128)} %bitcast.12, ...), custom_call_target="tpu_custom_call" | custom-call | tf_op jit(solution)/shard_map/layer/pallas_call | solution.py:478
  78.8 2.5 %finish.1 = (bf16[1,4096]{1,0:T(2,128)(2,1)}, bf16[3,16,512]{2,1,0:T(8,128)(2,1)}, f32[16,16,512]{2,1,0:T(8,128)}) custom-call(f32[1,4096]{1,0:T(1,128)} %get-tuple-element.9.row, bf16[3,16,512]{2,1,0:T(8,128)(2,1)} %get-tuple-element.10.ncs, f32[16,16,512]{2,1,0:T(8,128)} %get-tuple-element.11.nssm), custom_call_target="tpu_custom_call" | custom-call | tf_op jit(solution)/shard_map/finish/pallas_call | solution.py:553

commit v3 on v2

--- a/solution.py
+++ b/solution.py
@@ -11,18 +11,18 @@
 
 (
     PROJ, WOUT_M, WOUT, HID_M, HID, DOWN_M, MIX, MIX_M, OUTRED, RESID, STAT, SCALE,
-    ROWS1, ROWS2, ROWS3, ACT, RED1, RED2, FINAL, FINAL_M,
-) = range(20)
+    ROWS1, ROWS2, ROWS3, ACT, RED1, RED2, FINAL,
+) = range(19)
 
 
 def layer_kernel(
     x_hbm, z_hbm, cs_hbm, cw_hbm, cb_hbm, xw_hbm, dtb_hbm, alog_hbm, skip_hbm, gain_hbm, ids_hbm, rw_hbm, hid_hbm,
     dtw_hbm, ssm_hbm, ow_hbm, gate_hbm, up_hbm, down_hbm,
-    out_ref, ncs_hbm, nssm_hbm,
-    ncs_ref, nssm_ref, x_ref, z_ref, cs_ref, cw_ref, cb_ref, xw_ref, dtb_ref, alog_ref, skip_ref, gain_ref, ids_ref, rw_ref, hid_ref,
+    out_ref, ncs_ref, nssm_ref,
+    x_ref, z_ref, cs_ref, cw_ref, cb_ref, xw_ref, dtb_ref, alog_ref, skip_ref, gain_ref, ids_ref, rw_ref, hid_ref,
     dtw, ssm, wg, wu, wd, wd_mate, owh, ow,
     proj, proj_in, hid_out, hidh, hid_in, readout, mix, outb, outr, res, stat, scales, resrow, xn, acc_g, acc_u,
-    actw, act_mate, wrow, perm, own, red1, tsum, red2, vrow, vsend, final_in, fbuf, fmate,
+    actw, act_mate, wrow, perm, own, red1, tsum, red2, vrow, vsend, final_in,
     ssem, rsem, lsem,
 ):
     e = lax.axis_index("expert")
@@ -63,7 +63,7 @@
 
     early = [
         lcopy(src, dst, i) for i, (src, dst) in enumerate((
-            (x_hbm, x_ref), (cs_hbm, cs_ref), (cw_hbm, cw_ref), (cb_hbm, cb_ref), (xw_hbm, xw_ref),
+            (x_hbm, x_ref), (cs_hbm, cs_ref), (cw_hbm, cw_ref), (cb_hbm, cb_ref),
         ))
     ]
     later = [
@@ -82,6 +82,9 @@
 
     for s in range(2):
         weights.append(lcopy(down_cols(c, s), wd.at[s], 24 + s))
+    for k in range(4):
+        part = pl.ds(k * 128, 128 if k < 3 else 160)
+        early.append(lcopy(xw_hbm.at[part], xw_ref.at[part], 28 + k))
     own_weight = lcopy(ow_hbm.at[0, :, half(c)], owh.at[c], 15)
     for copy in early:
         copy.start()
@@ -139,6 +142,8 @@
 
     for copy in later:
         copy.start()
+    for copy in weights:
+        copy.start()
     for copy in later:
         copy.wait()
     hidden = hid_ref[...].astype(F32)
@@ -149,8 +154,6 @@
     ncs_ref[0] = cs_ref[1]
     ncs_ref[1] = cs_ref[2]
     ncs_ref[2] = x_ref[...]
-    ncs_copy = lcopy(ncs_ref, ncs_hbm, 26)
-    ncs_copy.start()
 
     ow[z] = owh[:, :, pl.ds(pl.multiple_of(z * 256, 256), 256)]
 
@@ -185,8 +188,6 @@
         new = jnp.exp(step_size[r : r + 1, :] * decay) * ssm[r] + driven[r : r + 1, :] * b_map[:, r : r + 1]
         nssm_ref[r] = new
         readout[r : r + 1, :] = jnp.sum(new * c_map[:, r : r + 1], axis=0, keepdims=True)
-    nssm_copy = lcopy(nssm_ref, nssm_hbm, 27)
-    nssm_copy.start()
     mix[e] = ((readout[...] + skip_ref[...] * inputs) * gate_z).astype(BF16)
 
     def mix_copy(o):
@@ -206,8 +207,6 @@
     hid_from_mate.wait_recv()
     others(8, z, lambda o: hid_copy(o).start())
     hid_in[z] = hidh[z]
-    for copy in weights:
-        copy.start()
     others(8, z, lambda o: wout_from(o).wait_recv())
 
     def mix_pass(o):
@@ -261,6 +260,12 @@
     def rows2_x(o, frm):
         return rcopy(xn.at[q1, :, x], xn.at[q1, :, frm], ROWS2, 4 + o, 4 + frm, at_x(o))
 
+    def pass_y(bx, o):
+        return rcopy(xn.at[q0, y, bx], xn.at[q0, y, bx], ROWS2, o, y, at_y(o))
+
+    def pass_x(by, o):
+        return rcopy(xn.at[q1, by, x], xn.at[q1, by, x], ROWS2, 4 + o, 4 + x, at_x(o))
+
     def rows3_0(q, o):
         return rcopy(xn.at[q, o], xn.at[q, o], ROWS3, o, o, (mate, t))
 
@@ -269,6 +274,8 @@
 
     others(4, x, lambda o: rows1_x(o, x).start())
     others(4, y, lambda o: rows1_y(o, y).start())
+    others(4, y, lambda o: pass_y(x, o).start())
+    others(4, x, lambda o: pass_x(y, o).start())
     squares = jnp.zeros((16, 256), F32)
     for b in range(8):
         piece = res[b].astype(F32)
@@ -290,12 +297,20 @@
     for k in range(2):
         mine = place == 2 * z + k
         for b in range(8):
-            resrow[k, b : b + 1, :] = jnp.sum(jnp.where(mine, res[b].astype(F32), 0.0), axis=0, keepdims=True)
-    others(4, x, lambda o: rows1_x(o, o).wait_recv())
-    others(4, y, lambda o: rows2_y(o, y).start())
+            line = jnp.sum(jnp.where(mine, res[b].astype(F32), 0.0), axis=0, keepdims=True)
+            resrow[k, 2 * b : 2 * b + 1, :] = line[:, 0:128]
+            resrow[k, 2 * b + 1 : 2 * b + 2, :] = line[:, 128:256]
+
+    def line_pass(d, carry):
+        bx, by = lax.rem(x + d, 4), lax.rem(y + d, 4)
+        rows1_x(bx, bx).wait_recv()
+        others(4, y, lambda o: pass_y(bx, o).start())
+        rows1_y(by, by).wait_recv()
+        others(4, x, lambda o: pass_x(by, o).start())
+        return carry
+
+    lax.fori_loop(1, 4, line_pass, 0)
     rows3_0(q0, y).start()
-    others(4, y, lambda o: rows1_y(o, o).wait_recv())
-    others(4, x, lambda o: rows2_x(o, x).start())
     rows3_1(q1, x).start()
     for copy in weights:
         copy.wait()
@@ -409,47 +424,33 @@
     for k in range(8):
         vrow[:, k, :] = first[:, 128 * k : 128 * (k + 1)]
         vrow[:, 8 + k, :] = second[:, 128 * k : 128 * (k + 1)]
-    vsend[...] = vrow[...].astype(BF16).reshape(8, 2, 16, 128)
+    vrow[pl.ds(2 * z, 2)] += resrow[...]
+    vsend[...] = vrow[...].astype(BF16)
 
     def final_copy(o):
-        return rcopy(vsend.at[o], final_in.at[z], FINAL, o, z, at_z(o))
-
-    others(8, z, lambda o: final_copy(o).start())
-    final_in[z] = vsend[z]
+        return rcopy(vsend.at[o], final_in.at[e], FINAL, o, e, (o, t))
+
+    others(16, e, lambda o: final_copy(o).start())
+    final_in[e] = vsend[e]
     others(4, y, lambda o: red2_y(o, y).wait_send())
     others(4, x, lambda o: red2_x(o, x).wait_send())
-    others(8, z, lambda o: rcopy(vsend.at[o], final_in.at[o], FINAL, o, o, at_z(o)).wait_recv())
-    rows = jnp.sum(final_in[...].astype(F32), axis=0)
+    others(16, e, lambda o: rcopy(vsend.at[o], final_in.at[o], FINAL, o, o, (o, t)).wait_recv())
     for k in range(2):
+        value = final_in[k].astype(F32)
+        for b in range(1, 8):
+            value = value + final_in[2 * b + k].astype(F32)
         for b in range(16):
-            tail = resrow[k, b // 2 : b // 2 + 1, (b % 2) * 128 : (b % 2 + 1) * 128]
-            fbuf[k, :, 128 * b : 128 * (b + 1)] = rows[k, b : b + 1, :] + tail
-    final_mate = rcopy(fbuf.at[m], fmate, FINAL_M, 0, 0, (mate, t))
-    final_mate.start()
-    out_ref[:, half(c)] = fbuf[c]
-    others(8, z, lambda o: final_copy(o).wait_send())
-    final_mate.wait()
-    ncs_copy.wait()
-    nssm_copy.wait()
-    out_ref[:, half(m)] = fmate[...]
-
-
-def finish_kernel(row, ncs, nssm, row_out, ncs_out, nssm_out, row_in, ncs_in, nssm_in, sem):
-    copies = [
-        pltpu.make_async_copy(src, dst, sem.at[k])
-        for k, (src, dst) in enumerate((
-            (nssm, nssm_in), (ncs, ncs_in), (row, row_in), (nssm_in, nssm_out), (ncs_in, ncs_out),
-        ))
-    ]
-    for k in range(3):
-        copies[k].start()
-    for k in range(2):
-        copies[k].wait()
-        copies[3 + k].start()
-    copies[2].wait()
-    row_out[...] = row_in[...].astype(BF16)
-    copies[3].wait()
-    copies[4].wait()
+            out_ref[:, 2048 * k + 128 * b : 2048 * k + 128 * (b + 1)] = value[b : b + 1, :]
+    others(16, e, lambda o: final_copy(o).wait_send())
+
+
+def finish_kernel(row, ncs, nssm, row_out, ncs_out, nssm_out, sem):
+    copies = [pltpu.make_async_copy(nssm, nssm_out, sem.at[0]), pltpu.make_async_copy(ncs, ncs_out, sem.at[1])]
+    for copy in copies:
+        copy.start()
+    row_out[...] = row[...].astype(BF16)
+    for copy in copies:
+        copy.wait()
 
 
 def local(
@@ -478,15 +479,13 @@
     row, new_conv_state, new_ssm_state = pl.pallas_call(
         layer_kernel,
         out_shape=(
-            jax.ShapeDtypeStruct((1, 4096), F32),
-            jax.ShapeDtypeStruct((3, 16, 512), BF16),
-            jax.ShapeDtypeStruct((16, 16, 512), F32),
+            pltpu.VMEM((1, 4096), F32),
+            pltpu.VMEM((3, 16, 512), BF16),
+            pltpu.VMEM((16, 16, 512), F32),
         ),
         in_specs=[hbm] * 19,
-        out_specs=(vmem, hbm, hbm),
+        out_specs=(vmem, vmem, vmem),
         scratch_shapes=[
-            pltpu.VMEM((3, 16, 512), BF16),
-            pltpu.VMEM((16, 16, 512), F32),
             pltpu.VMEM((16, 512), BF16),
             pltpu.VMEM((16, 512), BF16),
             pltpu.VMEM((3, 16, 512), BF16),
@@ -520,7 +519,7 @@
             pltpu.VMEM((8, 16, 256), BF16),
             pltpu.VMEM((2, 1, 128), F32),
             pltpu.VMEM((16, 1, 128), F32),
-            pltpu.VMEM((2, 8, 256), F32),
+            pltpu.VMEM((2, 16, 128), F32),
             pltpu.VMEM((4, 4, 4, 16, 1024), BF16),
             pltpu.VMEM((256, 384), F32),
             pltpu.VMEM((256, 384), F32),
@@ -533,23 +532,23 @@
             pltpu.VMEM((2, 4, 16, 1024), BF16),
             pltpu.VMEM((2, 4, 16, 1024), BF16),
             pltpu.VMEM((16, 16, 128), F32),
-            pltpu.VMEM((8, 2, 16, 128), BF16),
-            pltpu.VMEM((8, 2, 16, 128), BF16),
-            pltpu.VMEM((2, 1, 2048), F32),
-            pltpu.VMEM((1, 2048), F32),
-            pltpu.SemaphoreType.DMA((20, 16)),
-            pltpu.SemaphoreType.DMA((20, 16)),
-            pltpu.SemaphoreType.DMA((28,)),
+            pltpu.VMEM((16, 16, 128), BF16),
+            pltpu.VMEM((16, 16, 128), BF16),
+            pltpu.SemaphoreType.DMA((19, 16)),
+            pltpu.SemaphoreType.DMA((19, 16)),
+            pltpu.SemaphoreType.DMA((32,)),
         ],
         compiler_params=pltpu.CompilerParams(
-            collective_id=0, has_side_effects=True, vmem_limit_bytes=58 * 1024 * 1024
+            collective_id=0, has_side_effects=True, vmem_limit_bytes=48 * 1024 * 1024
         ),
         name="layer",
-    )(
-        x_stream, z_stream, conv_state.transpose(1, 0, 2), conv_weight, conv_bias[None], x_weight.T, dt_bias[None],
-        a_log, skip_gain[None], norm_gain[None], route_ids.T, route_weights.T, hidden_in,
-        dt_weight, ssm_state, out_weight, gate_proj, up_proj, down_proj,
-    )
+    )(*(
+        pltpu.with_memory_space_constraint(operand, pltpu.HBM) for operand in (
+            x_stream, z_stream, conv_state.transpose(1, 0, 2), conv_weight, conv_bias[None], x_weight.T,
+            dt_bias[None], a_log, skip_gain[None], norm_gain[None], route_ids.T, route_weights.T, hidden_in,
+            dt_weight, ssm_state, out_weight, gate_proj, up_proj, down_proj,
+        )
+    ))
     row, new_conv_state, new_ssm_state = pl.pallas_call(
         finish_kernel,
         out_shape=(
@@ -557,15 +556,10 @@
             jax.ShapeDtypeStruct((3, 16, 512), BF16),
             jax.ShapeDtypeStruct((16, 16, 512), F32),
         ),
-        in_specs=[hbm] * 3,
+        in_specs=[vmem] * 3,
         out_specs=(vmem, hbm, hbm),
-        scratch_shapes=[
-            pltpu.VMEM((1, 4096), F32),
-            pltpu.VMEM((3, 16, 512), BF16),
-            pltpu.VMEM((16, 16, 512), F32),
-            pltpu.SemaphoreType.DMA((5,)),
-        ],
-        compiler_params=pltpu.CompilerParams(vmem_limit_bytes=58 * 1024 * 1024),
+        scratch_shapes=[pltpu.SemaphoreType.DMA((2,))],
+        compiler_params=pltpu.CompilerParams(vmem_limit_bytes=48 * 1024 * 1024),
         name="finish",
     )(row, new_conv_state, new_ssm_state)
     return (row, new_conv_state.transpose(1, 0, 2), new_ssm_state)

time: 81.6 us -> 77.1 us (0.945)
  Pallas kernels: 80.7 us -> 76.2 us
    pallas_call x1, Pallas kernels: 78.2 us -> 74.8 us  [local(): pl.pallas_call(layer_kernel, out_shape=(pltpu.VMEM((1, 4096), F32), pltpu...]
    pallas_call x1, Pallas kernels: 2.48 us -> 1.42 us  [local(): pl.pallas_call(finish_kernel, out_shape=(jax.ShapeDtypeStruct((1, 4096),...]
where the time goes in v3:
time: 77.1 us; the launch traced here: 76.8 us
  Pallas kernels  76.2 us (99%)
    pallas_call x1, Pallas kernels, local(): pl.pallas_call(layer_kernel, out_shape=(pltpu.VMEM((1, 4096), F32), pltpu...  74.8 us

profile of v3, /device:TPU:1, one launch (start us, length us, event | category | flops | bytes accessed | tf_op | source)
XLA Modules:
  0.0 76.8 jit_solution(11094845561395338472)
XLA Ops:
  0.6 74.8 %layer.1 = (f32[1,4096]{1,0:T(1,128)S(1)}, bf16[3,16,512]{2,1,0:T(8,128)(2,1)S(1)}, f32[16,16,512]{2,1,0:T(8,128)S(1)}) custom-call(bf16[16,512]{1,0:T(8,128)(2,1)} %x_hbm.1, bf16[16,512]{1,0:T(8,128)(2,1)} %z_hbm.1, bf16[3,16,512]{2,1,0:T(8,128)(2,1)} %bitcast.10, bf16[4,512]{1,0:T(4,128)(2,1)} %cw_hbm.1, f32[1,512]{1,0:T(1,128)} %bitcast.12, ...), custom_call_target="tpu_custom_call" | custom-call | tf_op jit(solution)/shard_map/layer/pallas_call | solution.py:479
  75.4 1.4 %finish.1 = (bf16[1,4096]{1,0:T(2,128)(2,1)}, bf16[3,16,512]{2,1,0:T(8,128)(2,1)}, f32[16,16,512]{2,1,0:T(8,128)}) custom-call(f32[1,4096]{1,0:T(1,128)S(1)} %get-tuple-element.9.row, bf16[3,16,512]{2,1,0:T(8,128)(2,1)S(1)} %get-tuple-element.10.ncs, f32[16,16,512]{2,1,0:T(8,128)S(1)} %get-tuple-element.11.nssm), custom_call_target="tpu_custom_call" | custom-call | tf_op jit(solution)/shard_map/finish/pallas_call | solution.py:552

commit v4 on v3

--- a/solution.py
+++ b/solution.py
@@ -42,7 +42,7 @@
 
     def others(n, me, body):
         def step(d, carry):
-            body(lax.rem(me + d, n))
+            body(lax.rem(me + (5 * d if n == 16 else 3 * d if n == 8 else 3 - d + lax.div(d, 3) * 3), n))
             return carry
         lax.fori_loop(1, n, step, 0)
 
@@ -364,21 +364,29 @@
     act_copy = rcopy(actw, act_mate, ACT, 0, 0, (mate, t))
     act_copy.start()
 
-    def red1_x(o, frm):
-        return rcopy(own.at[0, :, o], red1.at[0, frm], RED1, o, frm, at_x(o))
-
-    def red1_y(o, frm):
-        return rcopy(own.at[1, o], red1.at[1, frm], RED1, 4 + o, 4 + frm, at_y(o))
-
-    value = jnp.dot(actw[...], wd[0], preferred_element_type=F32)
-    act_copy.wait()
-    value = value + jnp.dot(act_mate[...], wd_mate[0], preferred_element_type=F32)
-    own[0] = value.astype(BF16).reshape(4, 4, 16, 1024)
-    others(4, x, lambda o: red1_x(o, x).start())
-    value = jnp.dot(actw[...], wd[1], preferred_element_type=F32)
-    value = value + jnp.dot(act_mate[...], wd_mate[1], preferred_element_type=F32)
-    own[1] = value.astype(BF16).reshape(4, 4, 16, 1024)
-    others(4, y, lambda o: red1_y(o, y).start())
+    def red1_copy(s, h, o, frm):
+        if s == 0:
+            return rcopy(own.at[0, h, :, o], red1.at[0, h, frm], RED1, 4 * h + o, 4 * h + frm, at_x(o))
+        return rcopy(own.at[1, h, o], red1.at[1, h, frm], RED1, 8 + 4 * h + o, 8 + 4 * h + frm, at_y(o))
+
+    def red2_copy(s, h, o, frm):
+        if s == 0:
+            return rcopy(tsum.at[0, h, o], red2.at[0, h, frm], RED2, 4 * h + o, 4 * h + frm, at_y(o))
+        return rcopy(tsum.at[1, h, o], red2.at[1, h, frm], RED2, 8 + 4 * h + o, 8 + 4 * h + frm, at_x(o))
+
+    one, two = (x, y), (y, x)
+
+    def down(s, h, act, weight):
+        return jnp.dot(act[...], weight[s, :, 512 * h : 512 * (h + 1)], preferred_element_type=F32)
+
+    parts = [(0, 0), (1, 0), (0, 1), (1, 1)]
+    for s, h in parts:
+        value = down(s, h, actw, wd)
+        if (s, h) == (0, 0):
+            act_copy.wait()
+        value = value + down(s, h, act_mate, wd_mate)
+        own[s, h] = value.astype(BF16).reshape(4, 4, 16, 512)
+        others(4, one[s], lambda o: red1_copy(s, h, o, one[s]).start())
 
     others(16, t, lambda o: scale_copy(o).wait_send())
     others(4, y, lambda o: rows2_y(o, y).wait_send())
@@ -391,39 +399,24 @@
 
     lax.fori_loop(0, 4, rows3_sent, 0)
 
-    def red2_y(o, frm):
-        return rcopy(tsum.at[0, o], red2.at[0, frm], RED2, o, frm, at_y(o))
-
-    def red2_x(o, frm):
-        return rcopy(tsum.at[1, o], red2.at[1, frm], RED2, 4 + o, 4 + frm, at_x(o))
-
-    others(4, x, lambda o: red1_x(o, o).wait_recv())
-    value = own[0, :, x].astype(F32)
-    for d in range(1, 4):
-        value = value + red1[0, lax.rem(x + d, 4)].astype(F32)
-    tsum[0] = value.astype(BF16)
-    others(4, y, lambda o: red2_y(o, y).start())
-    others(4, y, lambda o: red1_y(o, o).wait_recv())
-    value = own[1, y].astype(F32)
-    for d in range(1, 4):
-        value = value + red1[1, lax.rem(y + d, 4)].astype(F32)
-    tsum[1] = value.astype(BF16)
-    others(4, x, lambda o: red2_x(o, x).start())
-    others(4, x, lambda o: red1_x(o, x).wait_send())
-    others(4, y, lambda o: red1_y(o, y).wait_send())
-
-    others(4, y, lambda o: red2_y(o, o).wait_recv())
-    first = tsum[0, y].astype(F32)
-    for d in range(1, 4):
-        first = first + red2[0, lax.rem(y + d, 4)].astype(F32)
-    others(4, x, lambda o: red2_x(o, o).wait_recv())
-    second = tsum[1, x].astype(F32)
-    for d in range(1, 4):
-        second = second + red2[1, lax.rem(x + d, 4)].astype(F32)
-
-    for k in range(8):
-        vrow[:, k, :] = first[:, 128 * k : 128 * (k + 1)]
-        vrow[:, 8 + k, :] = second[:, 128 * k : 128 * (k + 1)]
+    for s, h in parts:
+        others(4, one[s], lambda o: red1_copy(s, h, o, o).wait_recv())
+        value = (own[0, h, :, x] if s == 0 else own[1, h, y]).astype(F32)
+        for d in range(1, 4):
+            value = value + red1[s, h, lax.rem(one[s] + d, 4)].astype(F32)
+        tsum[s, h] = value.astype(BF16)
+        others(4, two[s], lambda o: red2_copy(s, h, o, two[s]).start())
+    for s, h in parts:
+        others(4, one[s], lambda o: red1_copy(s, h, o, one[s]).wait_send())
+
+    for s, h in parts:
+        others(4, two[s], lambda o: red2_copy(s, h, o, o).wait_recv())
+        value = tsum[s, h, two[s]].astype(F32)
+        for d in range(1, 4):
+            value = value + red2[s, h, lax.rem(two[s] + d, 4)].astype(F32)
+        for k in range(4):
+            vrow[:, 8 * s + 4 * h + k, :] = value[:, 128 * k : 128 * (k + 1)]
+
     vrow[pl.ds(2 * z, 2)] += resrow[...]
     vsend[...] = vrow[...].astype(BF16)
 
@@ -432,8 +425,8 @@
 
     others(16, e, lambda o: final_copy(o).start())
     final_in[e] = vsend[e]
-    others(4, y, lambda o: red2_y(o, y).wait_send())
-    others(4, x, lambda o: red2_x(o, x).wait_send())
+    for s, h in parts:
+        others(4, two[s], lambda o: red2_copy(s, h, o, two[s]).wait_send())
     others(16, e, lambda o: rcopy(vsend.at[o], final_in.at[o], FINAL, o, o, (o, t)).wait_recv())
     for k in range(2):
         value = final_in[k].astype(F32)
@@ -445,7 +438,10 @@
 
 
 def finish_kernel(row, ncs, nssm, row_out, ncs_out, nssm_out, sem):
-    copies = [pltpu.make_async_copy(nssm, nssm_out, sem.at[0]), pltpu.make_async_copy(ncs, ncs_out, sem.at[1])]
+    copies = [
+        pltpu.make_async_copy(nssm.at[pl.ds(4 * k, 4)], nssm_out.at[pl.ds(4 * k, 4)], sem.at[k]) for k in range(4)
+    ]
+    copies.append(pltpu.make_async_copy(ncs, ncs_out, sem.at[4]))
     for copy in copies:
         copy.start()
     row_out[...] = row[...].astype(BF16)
@@ -527,10 +523,10 @@
             pltpu.VMEM((256, 384), BF16),
             pltpu.VMEM((256, 128), F32),
             pltpu.VMEM((256, 256), BF16),
-            pltpu.VMEM((2, 4, 4, 16, 1024), BF16),
-            pltpu.VMEM((2, 4, 4, 16, 1024), BF16),
-            pltpu.VMEM((2, 4, 16, 1024), BF16),
-            pltpu.VMEM((2, 4, 16, 1024), BF16),
+            pltpu.VMEM((2, 2, 4, 4, 16, 512), BF16),
+            pltpu.VMEM((2, 2, 4, 4, 16, 512), BF16),
+            pltpu.VMEM((2, 2, 4, 16, 512), BF16),
+            pltpu.VMEM((2, 2, 4, 16, 512), BF16),
             pltpu.VMEM((16, 16, 128), F32),
             pltpu.VMEM((16, 16, 128), BF16),
             pltpu.VMEM((16, 16, 128), BF16),
@@ -558,7 +554,7 @@
         ),
         in_specs=[vmem] * 3,
         out_specs=(vmem, hbm, hbm),
-        scratch_shapes=[pltpu.SemaphoreType.DMA((2,))],
+        scratch_shapes=[pltpu.SemaphoreType.DMA((5,))],
         compiler_params=pltpu.CompilerParams(vmem_limit_bytes=48 * 1024 * 1024),
         name="finish",
     )(row, new_conv_state, new_ssm_state)

time: 77.1 us -> 74.9 us (0.971)
  Pallas kernels: 76.2 us -> 74 us
    pallas_call x1, Pallas kernels: 74.8 us -> 72.5 us  [local(): pl.pallas_call(layer_kernel, out_shape=(pltpu.VMEM((1, 4096), F32), pltpu...]
where the time goes in v4:
time: 74.9 us; the launch traced here: 74.6 us
  Pallas kernels  74 us (99%)
    pallas_call x1, Pallas kernels, local(): pl.pallas_call(layer_kernel, out_shape=(pltpu.VMEM((1, 4096), F32), pltpu...  72.5 us

profile of v4, /device:TPU:1, one launch (start us, length us, event | category | flops | bytes accessed | tf_op | source)
XLA Modules:
  0.0 74.6 jit_solution(3828661214365640018)
XLA Ops:
  0.6 72.5 %layer.1 = (f32[1,4096]{1,0:T(1,128)S(1)}, bf16[3,16,512]{2,1,0:T(8,128)(2,1)S(1)}, f32[16,16,512]{2,1,0:T(8,128)S(1)}) custom-call(bf16[16,512]{1,0:T(8,128)(2,1)} %x_hbm.1, bf16[16,512]{1,0:T(8,128)(2,1)} %z_hbm.1, bf16[3,16,512]{2,1,0:T(8,128)(2,1)} %bitcast.10, bf16[4,512]{1,0:T(4,128)(2,1)} %cw_hbm.1, f32[1,512]{1,0:T(1,128)} %bitcast.12, ...), custom_call_target="tpu_custom_call" | custom-call | tf_op jit(solution)/shard_map/layer/pallas_call | solution.py:475
  73.2 1.4 %finish.1 = (bf16[1,4096]{1,0:T(2,128)(2,1)}, bf16[3,16,512]{2,1,0:T(8,128)(2,1)}, f32[16,16,512]{2,1,0:T(8,128)}) custom-call(f32[1,4096]{1,0:T(1,128)S(1)} %get-tuple-element.9.row, bf16[3,16,512]{2,1,0:T(8,128)(2,1)S(1)} %get-tuple-element.10.ncs, f32[16,16,512]{2,1,0:T(8,128)S(1)} %get-tuple-element.11.nssm), custom_call_target="tpu_custom_call" | custom-call | tf_op jit(solution)/shard_map/finish/pallas_call | solution.py:548

commit v5 on v4

--- a/solution.py
+++ b/solution.py
@@ -302,7 +302,7 @@
             resrow[k, 2 * b + 1 : 2 * b + 2, :] = line[:, 128:256]
 
     def line_pass(d, carry):
-        bx, by = lax.rem(x + d, 4), lax.rem(y + d, 4)
+        bx, by = lax.rem(x + 4 - d, 4), lax.rem(y + 4 - d, 4)
         rows1_x(bx, bx).wait_recv()
         others(4, y, lambda o: pass_y(bx, o).start())
         rows1_y(by, by).wait_recv()
@@ -319,37 +319,37 @@
     others(4, x, lambda o: rows1_x(o, x).wait_send())
     others(4, y, lambda o: rows1_y(o, y).wait_send())
 
+    def forward(d, carry):
+        oy, ox = lax.rem(y + 4 - d, 4), lax.rem(x + 4 - d, 4)
+        rows2_y(oy, oy).wait_recv()
+        rows3_0(q0, oy).start()
+        rows2_x(ox, ox).wait_recv()
+        rows3_1(q1, ox).start()
+        return carry
+
+    lax.fori_loop(1, 4, forward, 0)
+
+    acc_g[...] = jnp.zeros((256, 384), F32)
+    acc_u[...] = jnp.zeros((256, 384), F32)
+
+    def project(q):
+        rows = xn[q].reshape(256, 1024)
+        acc_g[...] += jnp.dot(rows, wg[q], preferred_element_type=F32)
+        acc_u[...] += jnp.dot(rows, wu[q], preferred_element_type=F32)
+
+    def project_half(first):
+        def step(s, carry):
+            project(first + s)
+            return carry
+        lax.fori_loop(0, 2, step, 0)
+
+    project_half(q0)
+
     others(16, t, lambda o: rcopy(scales.at[o], scales.at[o], SCALE, o, o, (e, o)).wait_recv())
     lane = lax.broadcasted_iota(jnp.int32, (16, 16, 128), 2)
     slot = lax.broadcasted_iota(jnp.int32, (16, 16, 128), 1)
     picked = jnp.where(lane == slot, jnp.broadcast_to(scales[...], (16, 16, 128)), 0.0).reshape(256, 128)
     scale = jnp.broadcast_to(jnp.sum(picked, axis=1, keepdims=True), (256, 384))
-
-    def forward(d, carry):
-        oy, ox = lax.rem(y + d, 4), lax.rem(x + d, 4)
-        rows2_y(oy, oy).wait_recv()
-        rows3_0(q0, oy).start()
-        rows2_x(ox, ox).wait_recv()
-        rows3_1(q1, ox).start()
-        return carry
-
-    lax.fori_loop(1, 4, forward, 0)
-
-    acc_g[...] = jnp.zeros((256, 384), F32)
-    acc_u[...] = jnp.zeros((256, 384), F32)
-
-    def project(q):
-        rows = xn[q].reshape(256, 1024)
-        acc_g[...] += jnp.dot(rows, wg[q], preferred_element_type=F32)
-        acc_u[...] += jnp.dot(rows, wu[q], preferred_element_type=F32)
-
-    def project_half(first):
-        def step(s, carry):
-            project(first + s)
-            return carry
-        lax.fori_loop(0, 2, step, 0)
-
-    project_half(q0)
 
     def mate_rows(o, carry):
         rows3_0(p0, o).wait_recv()

time: 74.9 us -> 74.3 us (level)
  no operation moved by 1% of the time
where the time goes in v5:
time: 74.3 us; the launch traced here: 74.1 us
  Pallas kernels  73.4 us (99%)
    pallas_call x1, Pallas kernels, local(): pl.pallas_call(layer_kernel, out_shape=(pltpu.VMEM((1, 4096), F32), pltpu...  72 us

profile of v5, /device:TPU:1, one launch (start us, length us, event | category | flops | bytes accessed | tf_op | source)
XLA Modules:
  0.0 74.1 jit_solution(859309550173261363)
XLA Ops:
  0.6 72.0 %layer.1 = (f32[1,4096]{1,0:T(1,128)S(1)}, bf16[3,16,512]{2,1,0:T(8,128)(2,1)S(1)}, f32[16,16,512]{2,1,0:T(8,128)S(1)}) custom-call(bf16[16,512]{1,0:T(8,128)(2,1)} %x_hbm.1, bf16[16,512]{1,0:T(8,128)(2,1)} %z_hbm.1, bf16[3,16,512]{2,1,0:T(8,128)(2,1)} %bitcast.10, bf16[4,512]{1,0:T(4,128)(2,1)} %cw_hbm.1, f32[1,512]{1,0:T(1,128)} %bitcast.12, ...), custom_call_target="tpu_custom_call" | custom-call | tf_op jit(solution)/shard_map/layer/pallas_call | solution.py:475
  72.6 1.4 %finish.1 = (bf16[1,4096]{1,0:T(2,128)(2,1)}, bf16[3,16,512]{2,1,0:T(8,128)(2,1)}, f32[16,16,512]{2,1,0:T(8,128)}) custom-call(f32[1,4096]{1,0:T(1,128)S(1)} %get-tuple-element.9.row, bf16[3,16,512]{2,1,0:T(8,128)(2,1)S(1)} %get-tuple-element.10.ncs, f32[16,16,512]{2,1,0:T(8,128)S(1)} %get-tuple-element.11.nssm), custom_call_target="tpu_custom_call" | custom-call | tf_op jit(solution)/shard_map/finish/pallas_call | solution.py:548
